TPU v7x, 128 devices: a whole 4x4x4 slice. The times are simulated.
128 devices in a mesh: seq: 16 (over x, z_hi, core), fsdp: 4 (over y), dp: 2 (over z_lo).
Axes of the slice: x: 4, y: 4, z: 4 (z_hi: 2, z_lo: 2; z = z_hi * 2 + z_lo), core: 2. Of those that a mesh axis runs over, the one named last changes fastest.
Arguments:
- frames: bfloat16 [8, 6144, 1024], P(('fsdp', 'dp'), 'seq'), may hold values from -8 to 8
- utterance_valid_length: int32 [8], P(('fsdp', 'dp')), may hold values from 5376 to 6144, as said below
- utterance_span_frames: int32 [8], P(('fsdp', 'dp')), may hold values from 32 to 64, as said below
- upsampler_inproj: bfloat16 [1024, 3072], P('fsdp'), may hold values from -0.125 to 0.125
- upsampler_projection: bfloat16 [1024, 1024], P('fsdp'), may hold values from -0.1875 to 0.1875
- transformer_inproj: bfloat16 [1024, 3072], P('fsdp'), may hold values from -0.125 to 0.125
- transformer_projection: bfloat16 [1024, 1024], P('fsdp'), may hold values from -0.1875 to 0.1875
- cotangent: bfloat16 [8, 6144, 1024], P(('fsdp', 'dp'), 'seq'), may hold values from -6 to 6
Outputs:
- result: bfloat16 [8, 6144, 1024], P(('fsdp', 'dp'), 'seq')
- frame_input_gradient: bfloat16 [8, 6144, 1024], P(('fsdp', 'dp'), 'seq')
- upsampler_inproj_gradient: float32 [1024, 3072], P('fsdp')
- upsampler_projection_gradient: float32 [1024, 1024], P('fsdp')
- transformer_inproj_gradient: float32 [1024, 3072], P('fsdp')
- transformer_projection_gradient: float32 [1024, 1024], P('fsdp')
Inputs may be any that keep to these rules, and one draw needn't show every extreme that they name: Frames 0 to utterance_valid_length - 1 of each utterance are valid; some utterance has all 6144 frames valid. `utterance_span_frames`: some utterance uses spans of exactly 64 frames.
All inputs are finite; a program needn't handle non-finite values.
Results may differ from a plain program's by a relative error of at most 0.029.
Values may be sent and summed in bfloat16 or wider, within the bound.
A program may use at most 192 MiB of HBM per device.

v0:
```python
import math

import jax
import jax.numpy as jnp
from jax import lax
from jax.sharding import PartitionSpec as P

HEADS = 16
CMAX = 64


EPS = 1e-06


def from_behind(block, axis, distance):
    devices = range(lax.axis_size(axis))
    route = [(i - distance, i) for i in devices if i - distance in devices]
    return lax.ppermute(block, axis, route)


def normalize_rows(xfull):
    inverse = lax.rsqrt(jnp.mean(xfull * xfull, axis=-1, keepdims=True) + EPS)
    return (xfull * inverse, inverse)


def norm_backward(xfull, inverse, d_normed):
    row_inner = jnp.mean(d_normed * xfull, axis=-1, keepdims=True)
    return inverse * d_normed - xfull * (inverse * inverse * inverse) * row_inner


def span_window_mask(query_positions, key_positions, span_length, frame_length, behind, ahead):
    span_gap = key_positions[None, :] // span_length - query_positions[:, None] // span_length
    live_keys = (key_positions >= 0) & (key_positions < frame_length)
    return (span_gap >= -behind) & (span_gap <= ahead) & live_keys[None, :]


def attend_forward(query, keys, values, allowed, active_query):
    row_total, hidden_width = query.shape
    key_count = keys.shape[0]
    head_dim = hidden_width // HEADS
    query_heads = query.reshape(row_total, HEADS, head_dim)
    key_heads = keys.reshape(key_count, HEADS, head_dim)
    value_heads = values.reshape(key_count, HEADS, head_dim)
    scores = jnp.einsum(
        "rhd,ehd->hre", query_heads, key_heads, preferred_element_type=jnp.float32
    ) * head_dim ** (-0.5)
    scores = jnp.where(allowed[None], scores, -1e30)
    row_max = jnp.max(scores, axis=-1, keepdims=True)
    exp_terms = jnp.exp(scores - row_max)
    attn_prob = exp_terms / jnp.sum(exp_terms, axis=-1, keepdims=True)
    low_prob = attn_prob.astype(jnp.bfloat16)
    mixed = jnp.einsum("hre,ehd->rhd", low_prob, value_heads, preferred_element_type=jnp.float32)
    mixed = mixed * active_query[:, None, None]
    return (mixed.reshape(row_total, hidden_width).astype(jnp.bfloat16), attn_prob, low_prob)


def attend_backward(query, keys, values, attn_prob, low_prob, d_mixed):
    row_total, hidden_width = query.shape
    key_count = keys.shape[0]
    head_dim = hidden_width // HEADS
    query_heads = query.reshape(row_total, HEADS, head_dim)
    key_heads = keys.reshape(key_count, HEADS, head_dim)
    value_heads = values.reshape(key_count, HEADS, head_dim)
    d_heads = d_mixed.reshape(row_total, HEADS, head_dim)
    d_prob = jnp.einsum("rhd,ehd->hre", d_heads, value_heads, preferred_element_type=jnp.float32)
    row_inner = jnp.sum(attn_prob * d_prob, axis=-1, keepdims=True)
    d_score = (attn_prob * (d_prob - row_inner) * head_dim ** (-0.5)).astype(jnp.bfloat16)
    d_query = jnp.einsum("hre,ehd->rhd", d_score, key_heads, preferred_element_type=jnp.float32)
    d_key = jnp.einsum("hre,rhd->ehd", d_score, query_heads, preferred_element_type=jnp.float32)
    d_value = jnp.einsum("hre,rhd->ehd", low_prob, d_heads, preferred_element_type=jnp.float32)
    return (
        d_query.reshape(row_total, hidden_width),
        d_key.reshape(key_count, hidden_width),
        d_value.reshape(key_count, hidden_width),
    )


def block_partial(left, right):
    return (
        jnp.einsum("rd,re->de", left, right, preferred_element_type=jnp.float32)
        .astype(jnp.bfloat16)
        .astype(jnp.float32)
    )


def project_backward(grad_act, weight):
    return jnp.einsum("re,de->rd", grad_act, weight, preferred_element_type=jnp.float32)


def local(
    frames,
    utterance_valid_length,
    utterance_span_frames,
    upsampler_inproj,
    upsampler_projection,
    transformer_inproj,
    transformer_projection,
    cotangent,
):
    frame_rows = frames[0]
    gradient_row_block = cotangent[0]
    row_total, hidden_width = frame_rows.shape
    frame_length = utterance_valid_length[0]
    span_length = utterance_span_frames[0]
    rim_ahead = 2 * CMAX
    previous_border = 3 * CMAX
    first_frame = lax.axis_index("seq") * row_total
    local_positions = first_frame + jnp.arange(row_total, dtype=jnp.int32)
    ahead_pos = first_frame + jnp.arange(row_total + rim_ahead, dtype=jnp.int32)
    previous_positions = (
        first_frame - previous_border + jnp.arange(previous_border + row_total, dtype=jnp.int32)
    )
    active_query = (local_positions < frame_length).astype(jnp.float32)
    allowed_up = span_window_mask(local_positions, ahead_pos, span_length, frame_length, 0, 1)
    transformer_allowed = span_window_mask(
        local_positions, previous_positions, span_length, frame_length, 2, 0
    )
    (
        upsampler_inproj_weight,
        upsampler_projection_weight,
        transformer_inproj_weight,
        transformer_projection_weight,
    ) = (
        lax.all_gather(upsampler_inproj, "fsdp", axis=0, tiled=True),
        lax.all_gather(upsampler_projection, "fsdp", axis=0, tiled=True),
        lax.all_gather(transformer_inproj, "fsdp", axis=0, tiled=True),
        lax.all_gather(transformer_projection, "fsdp", axis=0, tiled=True),
    )
    xf_up = frame_rows.astype(jnp.float32)
    nf_up, inv_up = normalize_rows(xf_up)
    normed_up = nf_up.astype(jnp.bfloat16)
    act_up = jnp.dot(normed_up, upsampler_inproj_weight, preferred_element_type=jnp.float32).astype(
        jnp.bfloat16
    )
    query_up = act_up[:, :hidden_width]
    key_up = act_up[:, hidden_width : 2 * hidden_width]
    value_up = act_up[:, 2 * hidden_width :]
    ahead_key, ahead_value = from_behind((key_up[:rim_ahead], value_up[:rim_ahead]), "seq", -1)
    keys_up = jnp.concatenate([key_up, ahead_key], axis=0)
    values_up = jnp.concatenate([value_up, ahead_value], axis=0)
    mix_up, prob_up, low_up = attend_forward(query_up, keys_up, values_up, allowed_up, active_query)
    hidden_state = (
        xf_up + jnp.dot(mix_up, upsampler_projection_weight, preferred_element_type=jnp.float32)
    ).astype(jnp.bfloat16)
    transformer_frames = hidden_state.astype(jnp.float32)
    transformer_normed_frames, transformer_inverse_norm = normalize_rows(transformer_frames)
    transformer_normed = transformer_normed_frames.astype(jnp.bfloat16)
    transformer_activation = jnp.dot(
        transformer_normed, transformer_inproj_weight, preferred_element_type=jnp.float32
    ).astype(jnp.bfloat16)
    transformer_query = transformer_activation[:, :hidden_width]
    transformer_key = transformer_activation[:, hidden_width : 2 * hidden_width]
    transformer_value = transformer_activation[:, 2 * hidden_width :]
    previous_key, previous_value = from_behind(
        (
            transformer_key[row_total - previous_border :],
            transformer_value[row_total - previous_border :],
        ),
        "seq",
        1,
    )
    transformer_keys = jnp.concatenate([previous_key, transformer_key], axis=0)
    transformer_values = jnp.concatenate([previous_value, transformer_value], axis=0)
    transformer_mixed, transformer_probability, transformer_log_prob = attend_forward(
        transformer_query, transformer_keys, transformer_values, transformer_allowed, active_query
    )
    result = (
        transformer_frames
        + jnp.dot(
            transformer_mixed, transformer_projection_weight, preferred_element_type=jnp.float32
        )
    ).astype(jnp.bfloat16)
    transformer_mixed_gradient = (
        project_backward(gradient_row_block, transformer_projection_weight) * active_query[:, None]
    ).astype(jnp.bfloat16)
    transformer_projection_partial = block_partial(transformer_mixed, gradient_row_block)
    transformer_query_gradient, transformer_key_gradient, transformer_value_gradient = (
        attend_backward(
            transformer_query,
            transformer_keys,
            transformer_values,
            transformer_probability,
            transformer_log_prob,
            transformer_mixed_gradient,
        )
    )
    following_key, following_value = (
        from_behind(
            transformer_key_gradient[:previous_border].astype(jnp.bfloat16), "seq", -1
        ).astype(jnp.float32),
        from_behind(
            transformer_value_gradient[:previous_border].astype(jnp.bfloat16), "seq", -1
        ).astype(jnp.float32),
    )
    local_key_gradient = (
        transformer_key_gradient[previous_border:]
        .at[row_total - previous_border :]
        .add(following_key)
    )
    local_value_gradient = (
        transformer_value_gradient[previous_border:]
        .at[row_total - previous_border :]
        .add(following_value)
    )
    transformer_activation_gradient = jnp.concatenate(
        [transformer_query_gradient, local_key_gradient, local_value_gradient], axis=1
    ).astype(jnp.bfloat16)
    transformer_inproj_partial = block_partial(transformer_normed, transformer_activation_gradient)
    transformer_normed_gradient = project_backward(
        transformer_activation_gradient, transformer_inproj_weight
    )
    hidden_gradient = (
        gradient_row_block.astype(jnp.float32)
        + norm_backward(transformer_frames, transformer_inverse_norm, transformer_normed_gradient)
    ).astype(jnp.bfloat16)
    d_mix_up = (
        project_backward(hidden_gradient, upsampler_projection_weight) * active_query[:, None]
    ).astype(jnp.bfloat16)
    upsampler_projection_partial = block_partial(mix_up, hidden_gradient)
    dq_up, dk_up, dv_up = attend_backward(query_up, keys_up, values_up, prob_up, low_up, d_mix_up)
    earlier_key, earlier_value = (
        from_behind(dk_up[row_total:].astype(jnp.bfloat16), "seq", 1).astype(jnp.float32),
        from_behind(dv_up[row_total:].astype(jnp.bfloat16), "seq", 1).astype(jnp.float32),
    )
    dk_mine = dk_up[:row_total].at[:rim_ahead].add(earlier_key)
    dv_mine = dv_up[:row_total].at[:rim_ahead].add(earlier_value)
    dact_up = jnp.concatenate([dq_up, dk_mine, dv_mine], axis=1).astype(jnp.bfloat16)
    upsampler_inproj_partial = block_partial(normed_up, dact_up)
    dn_up = project_backward(dact_up, upsampler_inproj_weight)
    frame_input_gradient = (
        hidden_gradient.astype(jnp.float32) + norm_backward(xf_up, inv_up, dn_up)
    ).astype(jnp.bfloat16)
    softmax_scale = 1.0 / math.sqrt(
        lax.axis_size("seq") * lax.axis_size("fsdp") * lax.axis_size("dp") * row_total
    )
    shares = (
        lax.psum_scatter(
            upsampler_inproj_partial.astype(jnp.bfloat16), "fsdp", scatter_dimension=0, tiled=True
        ).astype(jnp.float32),
        lax.psum_scatter(
            upsampler_projection_partial.astype(jnp.bfloat16),
            "fsdp",
            scatter_dimension=0,
            tiled=True,
        ).astype(jnp.float32),
        lax.psum_scatter(
            transformer_inproj_partial.astype(jnp.bfloat16), "fsdp", scatter_dimension=0, tiled=True
        ).astype(jnp.float32),
        lax.psum_scatter(
            transformer_projection_partial.astype(jnp.bfloat16),
            "fsdp",
            scatter_dimension=0,
            tiled=True,
        ).astype(jnp.float32),
    )
    gradient_totals = (
        lax.psum(shares[0].astype(jnp.bfloat16), ("seq", "dp")).astype(jnp.float32),
        lax.psum(shares[1].astype(jnp.bfloat16), ("seq", "dp")).astype(jnp.float32),
        lax.psum(shares[2].astype(jnp.bfloat16), ("seq", "dp")).astype(jnp.float32),
        lax.psum(shares[3].astype(jnp.bfloat16), ("seq", "dp")).astype(jnp.float32),
    )
    upsampler_inproj_gradient = gradient_totals[0] * softmax_scale
    upsampler_projection_gradient = gradient_totals[1] * softmax_scale
    transformer_inproj_gradient = gradient_totals[2] * softmax_scale
    transformer_projection_gradient = gradient_totals[3] * softmax_scale
    return (
        result[None],
        frame_input_gradient[None],
        upsampler_inproj_gradient,
        upsampler_projection_gradient,
        transformer_inproj_gradient,
        transformer_projection_gradient,
    )


def solution(mesh):
    return jax.shard_map(
        local,
        mesh=mesh,
        in_specs=(
            P(("fsdp", "dp"), "seq", None),
            P(("fsdp", "dp")),
            P(("fsdp", "dp")),
            P("fsdp", None),
            P("fsdp", None),
            P("fsdp", None),
            P("fsdp", None),
            P(("fsdp", "dp"), "seq", None),
        ),
        out_specs=(
            P(("fsdp", "dp"), "seq", None),
            P(("fsdp", "dp"), "seq", None),
            P("fsdp", None),
            P("fsdp", None),
            P("fsdp", None),
            P("fsdp", None),
        ),
        check_vma=False,
    )
```

profile of v0, /device:TPU:1, one launch (start us, length us, event | category | flops | bytes accessed | tf_op | source)
XLA Modules:
  0.0 655.4 jit_solution(4947500784022818148)
XLA Ops:
  14.1 64.5 %all-gather.5.cloned.1.call-done = bf16[1024,3072]{1,0:T(8,128)(2,1)} async-done(((bf16[256,3072]{1,0:T(8,128)(2,1)}), bf16[1024,3072]{1,0:T(8,128)(2,1)}) %all-gather.5.cloned.1.call-update) | async-done | bytes 6291472 | tf_op jit(solution)/shard_map/all_gather | solution.py:124
  78.6 5.7 convolution_convert_fusion.3
  91.1 3.7 collective-permute-done.1
  94.8 2.9 collective-permute-done
  104.6 10.0 %fusion.125 = (f32[16,384]{1,0:T(8,128)S(1)}, f32[16,384,512]{2,1,0:T(8,128)}) fusion(pred[384,512]{1,0:T(8,128)(4,1)S(1)} %copy-done.23, bf16[384,16,64]{0,2,1:T(8,128)(2,1)S(1)} %bitcast.123, bf16[512,16,64]{0,2,1:T(8,128)(2,1)} %bitcast.120), kind=kOutput, calls=%fused_computation.163 | convolution fusion | flops 415236608 | bytes 14639104 | tf_op jit(solution)/shard_map/sub | solution.py:49
  114.6 5.8 multiply_convert_fusion.5
  120.5 3.0 fusion.52
  123.5 55.8 %all-gather.9.cloned.1.call-done = bf16[1024,3072]{1,0:T(8,128)(2,1)} async-done(((bf16[256,3072]{1,0:T(8,128)(2,1)}), bf16[1024,3072]{1,0:T(8,128)(2,1)}) %all-gather.9.cloned.1.call-update) | async-done | bytes 6291472 | tf_op jit(solution)/shard_map/all_gather | solution.py:126
  179.2 5.7 convolution_convert_fusion.2
  185.8 5.4 collective-permute-start.3
  203.0 9.0 %fusion.126 = (f32[16,384]{1,0:T(8,128)S(1)}, f32[16,384,576]{1,2,0:T(8,128)}) fusion(pred[384,576]{0,1:T(8,128)(4,1)S(1)} %copy-done.22, bf16[384,16,64]{0,2,1:T(8,128)(2,1)} %bitcast.124, bf16[576,16,64]{0,2,1:T(8,128)(2,1)} %bitcast.116), kind=kOutput, calls=%fused_computation.164 | convolution fusion | flops 467141184 | bytes 16367616 | tf_op jit(solution)/shard_map/sub | solution.py:49
  212.0 8.0 %multiply_convert_fusion.4 = bf16[16,64,384]{2,1,0:T(8,128)(2,1)} fusion(bf16[576,16,64]{0,2,1:T(8,128)(2,1)S(1)} %bitcast.108, f32[384]{0:T(512)S(1)} %copy-done.29, f32[16,384]{1,0:T(8,128)S(1)} %get-tuple-element.76, pred[384,576]{0,1:T(8,128)(4,1)S(1)} %copy-done.22, bf16[384,16,64]{0,2,1:T(8,128)(2,1)S(1)} %bitcast.127, bf16[576,16,64]{0,2,1:T(8,128)(2,1)} %bitcast.117), kind=kOutput, calls=%fused_computation.79 | convolution fusion | flops 924457536 | bytes 4179456 | tf_op jit(solution)/shard_map/hre,ehd->rhd/dot_general | solution.py:52
  219.9 4.0 convolution_convert_fusion.4
  224.5 3.5 multiply_convert_fusion.3
  229.5 9.0 %fusion.40 = f32[576,16,64]{0,2,1:T(8,128)} fusion(bf16[384,16,64]{0,2,1:T(8,128)(2,1)S(1)} %bitcast.112, f32[16,384]{1,0:T(8,128)S(1)} %get-tuple-element.76, pred[384,576]{0,1:T(8,128)(4,1)S(1)} %copy-done.22, bf16[384,16,64]{0,2,1:T(8,128)(2,1)} %bitcast.125, bf16[576,16,64]{0,2,1:T(8,128)(2,1)} %bitcast.118), kind=kOutput, calls=%fused_computation.57 | convolution fusion | flops 923671104 | bytes 5357568 | tf_op jit(solution)/shard_map/hre,rhd->ehd/dot_general | solution.py:70
  242.5 6.4 fusion.127
  248.9 19.7 %fusion.43 = f32[576,16,64]{0,2,1:T(8,128)S(1)} fusion(bf16[384,16,64]{0,2,1:T(8,128)(2,1)} %bitcast.126, f32[16,384,576]{1,2,0:T(8,128)} %fusion.127, f32[16,384,576]{1,2,0:T(8,128)} %get-tuple-element.77, f32[16,384]{1,0:T(8,128)S(1)} %get-tuple-element.76), kind=kOutput, calls=%fused_computation.58 | convolution fusion | flops 477764160 | bytes 31481856 | tf_op jit(solution)/shard_map/hre,rhd->ehd/dot_general | solution.py:69
  271.7 20.5 %fusion.75 = bf16[16,64,384]{2,1,0:T(8,128)(2,1)} fusion(bf16[576,16,64]{0,2,1:T(8,128)(2,1)} %bitcast.119, f32[16,384,576]{1,2,0:T(8,128)} %fusion.127, f32[16,384,576]{1,2,0:T(8,128)} %get-tuple-element.77, f32[16,384]{1,0:T(8,128)S(1)} %get-tuple-element.76), kind=kOutput, calls=%fused_computation.82 | convolution fusion | flops 478157376 | bytes 30302208 | tf_op jit(solution)/shard_map/hre,ehd->rhd/dot_general | solution.py:68
  297.7 5.6 scatter-add.15
  304.7 4.7 scatter-add.14
  309.4 6.1 fusion.59
  319.2 6.8 %convolution_convert_fusion = bf16[1024,3072]{1,0:T(8,128)(2,1)} fusion(bf16[384,1024]{0,1:T(8,128)(2,1)S(1)} %copy-done.13, bf16[384,1024]{0,1:T(8,128)(2,1)S(1)} %scatter-add.14, bf16[384,1024]{0,1:T(8,128)(2,1)} %bitcast.139, bf16[384,1024]{1,0:T(8,128)(2,1)S(1)} %get-tuple-element.75, f32[384]{0:T(512)S(1)} %get-tuple-element.71), kind=kOutput, calls=%fused_computation.28 | convolution fusion | flops 2427322368 | bytes 9438720 | tf_op jit(solution)/shard_map/rd,re->de/dot_general | solution.py:80
  329.1 5.9 fusion.46
  337.0 6.0 collective-permute-start.7
  343.1 6.3 fusion.128
  349.4 51.8 %fusion.49 = f32[512,16,64]{0,2,1:T(8,128)} fusion(bf16[384,16,64]{0,2,1:T(8,128)(2,1)} %bitcast.122, f32[16,384,512]{2,1,0:T(8,128)} %fusion.128, f32[16,384,512]{2,1,0:T(8,128)} %get-tuple-element.73, f32[16,384]{1,0:T(8,128)S(1)} %copy-done.33), kind=kOutput, calls=%fused_computation.60 | convolution fusion | flops 424679936 | bytes 28073984 | tf_op jit(solution)/shard_map/hre,rhd->ehd/dot_general | solution.py:69
  405.4 40.9 %fusion.72 = bf16[16,64,384]{2,1,0:T(8,128)(2,1)} fusion(bf16[512,16,64]{0,2,1:T(8,128)(2,1)S(1)} %bitcast.121, f32[16,384,512]{2,1,0:T(8,128)} %fusion.128, f32[16,384,512]{2,1,0:T(8,128)} %get-tuple-element.73, f32[16,384]{1,0:T(8,128)S(1)} %copy-done.33), kind=kOutput, calls=%fused_computation.81 | convolution fusion | flops 425073152 | bytes 27025408 | tf_op jit(solution)/shard_map/hre,ehd->rhd/dot_general | solution.py:68
  450.9 8.4 %convolution_convert_fusion.1 = bf16[1024,3072]{1,0:T(8,128)(2,1)} fusion(bf16[384,1024]{0,1:T(8,128)(2,1)S(1)} %constant_dynamic-update-slice_fusion, bf16[384,1024]{0,1:T(8,128)(2,1)S(1)} %constant_dynamic-update-slice_fusion.1, bf16[384,1024]{0,1:T(8,128)(2,1)S(1)} %bitcast.136, bf16[1,384,1024]{2,1,0:T(8,128)(2,1)S(1)} %copy-done.1, f32[384]{0:T(512)S(1)} %copy-done.26), kind=kOutput, calls=%fused_computation.29 | convolution fusion | flops 2427322368 | bytes 9438720 | tf_op jit(solution)/shard_map/rd,re->de/dot_general | solution.py:80
  459.4 65.0 %reduce-scatter.5.cloned.1.call-done = bf16[256,3072]{1,0:T(8,128)(2,1)} async-done(((bf16[1024,3072]{1,0:T(8,128)(2,1)}), bf16[256,3072]{1,0:T(8,128)(2,1)}) %reduce-scatter.5.cloned.1.call-update) | async-done | bytes 1572880 | tf_op jit(solution)/shard_map/reduce_scatter | solution.py:237
  524.4 3.8 fusion.78
  528.3 5.6 fusion.67
  535.2 104.7 %all-reduce.3.cloned.1.call-done = (bf16[256,3072]{1,0:T(8,128)(2,1)}, bf16[256,1024]{1,0:T(8,128)(2,1)}, bf16[256,3072]{1,0:T(8,128)(2,1)}, bf16[256,1024]{1,0:T(8,128)(2,1)}) async-done(((bf16[256,3072]{1,0:T(8,128)(2,1)}, bf16[256,1024]{1,0:T(8,128)(2,1)}, bf16[256,3072]{1,0:T(8,128)(2,1)}, bf16[256,1024]{1,0:T(8,128)(2,1)}), (bf16[256,3072]{1,0:T(8,128)(2,1)}, bf16[256,1024]{1,0:T(8,128)(2,1)}, ...) | async-done | bytes 4194320 | tf_op jit(solution)/shard_map/psum | solution.py:257
  (159 shorter events, 75.1 us)
Async XLA Ops:
  7.2 71.4 %all-gather.5.cloned.1.call-start = ((), (), s32[]{:S(2)}) async-start(), calls=%async_computation.4 | async-start | bytes 7864320 | tf_op jit(solution)/shard_map/all_gather | solution.py:124
  7.9 112.5 %all-gather.7.cloned.1.call-start = ((), (), s32[]{:S(2)}) async-start(), calls=%async_computation.5 | async-start | bytes 2621440 | tf_op jit(solution)/shard_map/all_gather | solution.py:125
  8.7 170.5 %all-gather.9.cloned.1.call-start = ((), (), s32[]{:S(2)}) async-start(), calls=%async_computation.6 | async-start | bytes 7864320 | tf_op jit(solution)/shard_map/all_gather | solution.py:126
  9.4 215.1 %all-gather.11.cloned.1.call-start = ((), (), s32[]{:S(2)}) async-start(), calls=%async_computation.7 | async-start | bytes 2621440 | tf_op jit(solution)/shard_map/all_gather | solution.py:127
  10.0 449.4 %reduce-scatter.11.cloned.1.call-start = ((), (), s32[]{:S(2)}) async-start(), calls=%async_computation.11 | async-start | bytes 2621440 | tf_op jit(solution)/shard_map/reduce_scatter | solution.py:249
  11.3 103.2 %copy-start.28 = (f32[384]{0:T(512)}, f32[384]{0:T(512)S(1)}, u32[]{:S(2)}) copy-start(f32[384]{0:T(512)S(1)} %fusion.104) | copy-start | bytes 4612
  12.5 71.9 %copy-start.25 = (f32[384]{0:T(512)}, f32[384]{0:T(512)S(1)}, u32[]{:S(2)}) copy-start(f32[384]{0:T(512)S(1)} %get-tuple-element.69) | copy-start | bytes 4612
  85.2 9.6 %collective-permute-start.1 = (bf16[128,1024]{1,0:T(8,128)(2,1)}, bf16[128,1024]{1,0:T(8,128)(2,1)S(1)}, u32[]{:S(2)}, u32[]{:S(2)}) collective-permute-start(bf16[128,1024]{1,0:T(8,128)(2,1)} %get-tuple-element.66), channel_id=1, source_target_pairs={{8,0},{16,8},{24,16},{32,24},{40,32},{48,40},{56,48},{64,56},{72,6... | collective-permute-start | bytes 786440 | tf_op jit(solution)/shard_map/ppermute | solution.py:18
  87.8 9.9 %collective-permute-start = (bf16[128,1024]{1,0:T(8,128)(2,1)}, bf16[128,1024]{1,0:T(8,128)(2,1)}, u32[]{:S(2)}, u32[]{:S(2)}) collective-permute-start(bf16[128,1024]{1,0:T(8,128)(2,1)} %get-tuple-element.67), channel_id=1, source_target_pairs={{8,0},{16,8},{24,16},{32,24},{40,32},{48,40},{56,48},{64,56},{72,6... | collective-permute-start | bytes 786440 | tf_op jit(solution)/shard_map/ppermute | solution.py:18
  97.7 6.9 %copy-start.10 = (bf16[384,1024]{0,1:T(8,128)(2,1)S(1)}, bf16[384,1024]{0,1:T(8,128)(2,1)}, u32[]{:S(2)}) copy-start(bf16[384,1024]{0,1:T(8,128)(2,1)} %copy.31) | copy-start | bytes 2359300
  101.9 12.7 %copy-start.2 = (bf16[512,1024]{0,1:T(8,128)(2,1)}, bf16[512,1024]{0,1:T(8,128)(2,1)S(1)}, u32[]{:S(2)}) copy-start(bf16[512,1024]{0,1:T(8,128)(2,1)S(1)} %copy.30) | copy-start | bytes 3145732
  120.4 64.5 %copy-start.18 = (bf16[16,64,384]{2,1,0:T(8,128)(2,1)}, bf16[16,64,384]{2,1,0:T(8,128)(2,1)S(1)}, u32[]{:S(2)}) copy-start(bf16[16,64,384]{2,1,0:T(8,128)(2,1)S(1)} %multiply_convert_fusion.5) | copy-start | bytes 2359300
  179.2 11.9 %copy-start.27 = (pred[576]{0:T(1024)(128)(4,1)S(1)}, pred[576]{0:T(1024)(128)(4,1)}, u32[]{:S(2)}) copy-start(pred[576]{0:T(1024)(128)(4,1)} %fusion.97) | copy-start | bytes 1732
  185.8 10.7 %collective-permute-start.3 = (bf16[192,1024]{1,0:T(8,128)(2,1)S(1)}, bf16[192,1024]{1,0:T(8,128)(2,1)S(1)}, u32[]{:S(2)}, u32[]{:S(2)}) collective-permute-start(bf16[192,1024]{1,0:T(8,128)(2,1)S(1)} %get-tuple-element.58), channel_id=1, source_target_pairs={{0,8},{8,16},{16,24},{24,32},{32,40},{40,48},{48,56},{56,64},{64,7... | collective-permute-start | bytes 1179656 | tf_op jit(solution)/shard_map/ppermute | solution.py:18
  192.1 8.0 %collective-permute-start.2 = (bf16[192,1024]{1,0:T(8,128)(2,1)}, bf16[192,1024]{1,0:T(8,128)(2,1)S(1)}, u32[]{:S(2)}, u32[]{:S(2)}) collective-permute-start(bf16[192,1024]{1,0:T(8,128)(2,1)} %get-tuple-element.59), channel_id=1, source_target_pairs={{0,8},{8,16},{16,24},{24,32},{32,40},{40,48},{48,56},{56,64},{64,7... | collective-permute-start | bytes 1179656 | tf_op jit(solution)/shard_map/ppermute | solution.py:18
  196.6 6.4 copy-start.22
  203.0 9.0 %copy-start.11 = (bf16[384,1024]{0,1:T(8,128)(2,1)S(1)}, bf16[384,1024]{0,1:T(8,128)(2,1)}, u32[]{:S(2)}) copy-start(bf16[384,1024]{0,1:T(8,128)(2,1)} %copy.34) | copy-start | bytes 2359300
  203.0 9.0 %copy-start.29 = (f32[384]{0:T(512)S(1)}, f32[384]{0:T(512)}, u32[]{:S(2)}) copy-start(f32[384]{0:T(512)} %copy-done.28) | copy-start | bytes 4612
  224.0 235.4 %reduce-scatter.7.cloned.1.call-start = ((), (), s32[]{:S(2)}) async-start(), calls=%async_computation.9 | async-start | bytes 2621440 | tf_op jit(solution)/shard_map/reduce_scatter | solution.py:240
  240.6 55.7 %collective-permute-start.5 = (bf16[192,1024]{0,1:T(8,128)(2,1)}, bf16[192,1024]{0,1:T(8,128)(2,1)}, u32[]{:S(2)}, u32[]{:S(2)}) collective-permute-start(bf16[192,1024]{0,1:T(8,128)(2,1)} %bitcast.26), channel_id=1, source_target_pairs={{8,0},{16,8},{24,16},{32,24},{40,32},{48,40},{56,48},{64,56},{72,6... | collective-permute-start | bytes 1179656 | tf_op jit(solution)/shard_map/ppermute | solution.py:18
  268.6 27.7 %copy-start.4 = (f32[576,16,64]{0,2,1:T(8,128)}, f32[576,16,64]{0,2,1:T(8,128)S(1)}, u32[]{:S(2)}) copy-start(f32[576,16,64]{0,2,1:T(8,128)S(1)} %fusion.43) | copy-start | bytes 7077892
  269.6 33.8 %collective-permute-start.4 = (bf16[192,1024]{0,1:T(8,128)(2,1)}, bf16[192,1024]{0,1:T(8,128)(2,1)}, u32[]{:S(2)}, u32[]{:S(2)}) collective-permute-start(bf16[192,1024]{0,1:T(8,128)(2,1)} %bitcast.22), channel_id=1, source_target_pairs={{8,0},{16,8},{24,16},{32,24},{40,32},{48,40},{56,48},{64,56},{72,6... | collective-permute-start | bytes 1179656 | tf_op jit(solution)/shard_map/ppermute | solution.py:18
  296.3 7.0 %slice-start = ((f32[576,16,64]{0,2,1:T(8,128)}), f32[192,16,64]{0,2,1:T(8,128)S(1)}, s32[]{:S(2)}) async-start(f32[576,16,64]{0,2,1:T(8,128)} %copy-done.4), calls=%async_computation.13 | async-start | bytes 2097152 | tf_op jit(solution)/shard_map/slice.98
  296.3 8.3 %copy-start.12 = (bf16[384,16,64]{0,2,1:T(8,128)(2,1)S(1)}, bf16[384,16,64]{0,2,1:T(8,128)(2,1)}, u32[]{:S(2)}) copy-start(bf16[384,16,64]{0,2,1:T(8,128)(2,1)} %slice.198) | copy-start | bytes 2359300
  309.3 6.1 copy-start.17
  319.1 140.3 %reduce-scatter.9.cloned.1.call-start = ((), (), s32[]{:S(2)}) async-start(), calls=%async_computation.10 | async-start | bytes 7864320 | tf_op jit(solution)/shard_map/reduce_scatter | solution.py:246
  326.0 198.4 %reduce-scatter.5.cloned.1.call-start = ((), (), s32[]{:S(2)}) async-start(), calls=%async_computation.8 | async-start | bytes 7864320 | tf_op jit(solution)/shard_map/reduce_scatter | solution.py:237
  329.0 14.0 %copy-start.3 = (bf16[512,1024]{0,1:T(8,128)(2,1)S(1)}, bf16[512,1024]{0,1:T(8,128)(2,1)}, u32[]{:S(2)}) copy-start(bf16[512,1024]{0,1:T(8,128)(2,1)} %copy-done.2) | copy-start | bytes 3145732
  337.0 111.5 %collective-permute-start.7 = (bf16[128,1024]{0,1:T(8,128)(2,1)}, bf16[128,1024]{0,1:T(8,128)(2,1)}, u32[]{:S(2)}, u32[]{:S(2)}) collective-permute-start(bf16[128,1024]{0,1:T(8,128)(2,1)} %bitcast.37), channel_id=1, source_target_pairs={{0,8},{8,16},{16,24},{24,32},{32,40},{40,48},{48,56},{56,64},{64,7... | collective-permute-start | bytes 786440 | tf_op jit(solution)/shard_map/ppermute | solution.py:18
  349.4 56.0 %copy-start.9 = (bf16[512,1024]{0,1:T(8,128)(2,1)S(1)}, bf16[512,1024]{0,1:T(8,128)(2,1)}, u32[]{:S(2)}) copy-start(bf16[512,1024]{0,1:T(8,128)(2,1)} %copy.32) | copy-start | bytes 3145732
  403.0 46.6 %collective-permute-start.6 = (bf16[128,1024]{0,1:T(8,128)(2,1)}, bf16[128,1024]{0,1:T(8,128)(2,1)}, u32[]{:S(2)}, u32[]{:S(2)}) collective-permute-start(bf16[128,1024]{0,1:T(8,128)(2,1)} %bitcast.33), channel_id=1, source_target_pairs={{0,8},{8,16},{16,24},{24,32},{32,40},{40,48},{48,56},{56,64},{64,7... | collective-permute-start | bytes 786440 | tf_op jit(solution)/shard_map/ppermute | solution.py:18
  459.3 180.6 %all-reduce.3.cloned.1.call-start = ((), (), s32[]{:S(2)}) async-start(), calls=%async_computation.12 | async-start | bytes 8388608 | tf_op jit(solution)/shard_map/psum | solution.py:257
  (23 other events, 79.6 us)
Sparse Core Ops, SparseCore 0:
  9.7 68.8 all-gather.4
  80.3 31.5 all-gather.6
  113.5 65.6 all-gather.8
  180.7 31.5 all-gather.10
  224.1 30.8 reduce-scatter.10
  319.3 32.7 reduce-scatter.6
  354.5 63.6 reduce-scatter.8
  459.4 64.9 reduce-scatter.4
  528.1 111.7 all-reduce.2
where the time goes:
time: 665 us; the launch traced here: 655 us
  waiting for transfers between devices  301 us (45%)
  matrix products  251 us (38%)
  local copies, waits for them, and re-layouts  38.5 us (6%)
  starting transfers between devices  25.1 us (4%)
  other arithmetic  23.1 us (3%)
  between operations  16.2 us (2%)
    psum x1, waiting for transfers between devices, local(): lax.psum(shares[0].astype(jnp.bfloat16), ('seq', 'dp')).astype(jnp.float32)  105 us
    dot_general x2, matrix products, attend_backward(): jnp.einsum('hre,rhd->ehd', d_score, query_heads, preferred_element_type=j...  71.5 us
    reduce_scatter x1, waiting for transfers between devices, local(): lax.psum_scatter(upsampler_inproj_partial.astype(jnp.bfloat16), 'fsdp', s...  65 us
    all_gather x1, waiting for transfers between devices, local(): lax.all_gather(upsampler_inproj, 'fsdp', axis=0, tiled=True)  64.5 us
    dot_general x2, matrix products, attend_backward(): jnp.einsum('hre,ehd->rhd', d_score, key_heads, preferred_element_type=jnp...  61.4 us
    all_gather x1, waiting for transfers between devices, local(): lax.all_gather(transformer_inproj, 'fsdp', axis=0, tiled=True)  55.8 us
    ppermute x8, starting transfers between devices, from_behind(): return lax.ppermute(block, axis, route)  24.4 us
    dot_general x4, matrix products, block_partial(): jnp.einsum('rd,re->de', left, right, preferred_element_type=jnp.float32)  21.8 us
  transfers between devices with their start and end apart: 17, of which 7 were waited for; matrix products, arithmetic and copies ran while one was open for 46% of the time, Pallas kernels for 0%

commit v1 on v0

v1 whole, which is shorter than its diff:
```python
import functools
import jax
import jax.numpy as jnp
from jax import lax
from jax.experimental import pallas as pl
from jax.experimental.pallas import tpu as pltpu
from jax.sharding import PartitionSpec as P

LINKS = ("xA", "yB", "zA", "xB", "yA", "zB")
PLANE = ("xA", "zA", "xB", "zB")


class Place:
    def __init__(self):
        seq = lax.axis_index("seq")
        self.y = lax.axis_index("fsdp")
        self.zl = lax.axis_index("dp")
        self.x = seq // 4
        self.zh = (seq // 2) % 2
        self.c = seq % 2
        self.z = self.zh * 2 + self.zl

    def bit(self, link):
        p = {"x": self.x, "y": self.y, "z": self.z}[link[0]]
        return ((p + 1) // 2) % 2 if link[1] == "A" else p // 2

    def peer(self, link):
        x, y, z, c = self.x, self.y, self.z, self.c
        if link == "core":
            c = 1 - c
        elif link[0] == "x":
            x = 3 - x if link[1] == "B" else x + 1 - 2 * (x % 2)
        elif link[0] == "y":
            y = 3 - y if link[1] == "B" else y + 1 - 2 * (y % 2)
        else:
            z = 3 - z if link[1] == "B" else z + 1 - 2 * (z % 2)
        return {"seq": x * 4 + (z // 2) * 2 + c, "fsdp": y, "dp": z % 2}


def greet(me):
    barrier = pltpu.get_barrier_semaphore()
    for link in LINKS + ("core",):
        pl.semaphore_signal(barrier, inc=1, device_id=me.peer(link), device_id_type=pl.DeviceIdType.MESH)
    pl.semaphore_wait(barrier, 7)


class Sems:
    def __init__(self, send, recv):
        self.send, self.recv, self.n = send, recv, 0

    def copy(self, me, link, src, dst):
        k = self.n
        self.n += 1
        return pltpu.make_async_remote_copy(
            src_ref=src, dst_ref=dst, send_sem=self.send.at[k], recv_sem=self.recv.at[k],
            device_id=me.peer(link), device_id_type=pl.DeviceIdType.MESH)


def rows(block, off, count):
    return pl.ds(pl.multiple_of(block * 256 + off, 16), count)


class Gather:
    def __init__(self, me, sems, shard, full, width, at, order):
        self.me, self.sems, self.shard, self.full, self.order = me, sems, shard, full, order
        self.cols = pl.ds(pl.multiple_of(at, 128), width)
        self.sent = []
        y = me.y
        self.a, self.b = y + 1 - 2 * (y % 2), 3 - y
        self.ab = 3 - self.a
        self.steps = len(order) + 1
        self.span = 16 if len(order) > 2 else 256
        self.off = 0
        if len(order) > 2:
            for k, link in enumerate(order[2:]):
                self.off = self.off + me.bit(link) * (16 << k)
        self.wait_for = []

    def own(self):
        return self.shard.at[pl.ds(pl.multiple_of(self.off + 0, 16), self.span), self.cols]

    def blk(self, block):
        return self.full.at[rows(block, self.off, self.span), self.cols]

    def _go(self, link, pairs):
        made = [self.sems.copy(self.me, link, s, d) for s, d in pairs]
        for m in made:
            m.start()
        self.sent += made
        self.wait_for = made

    def start(self, step):
        me = self.me
        if step < 2:
            link = self.order[step]
            pairs = [(self.own(), self.blk(me.y))]
            if step == 1:
                other = self.a if self.order[0] == "yA" else self.b
                pairs.append((self.blk(other), self.blk(other)))
            self._go(link, pairs)
        elif step < len(self.order):
            self._go(self.order[step], [(self.blk(k), self.blk(k)) for k in (self.a, self.b, self.ab)])
        else:
            self._go("core", [(self.blk(k), self.blk(k)) for k in (self.a, self.b, self.ab)])

    def finish(self, step):
        for m in self.wait_for:
            m.wait_recv()
        if 2 <= step < len(self.order):
            link = self.order[step]
            self.off = self.off - self.me.bit(link) * self.span
            self.span *= 2

    def close(self):
        for m in self.sent:
            m.wait_send()


class Reduce:
    def __init__(self, me, sems, terms, acc, inbox, inbox_core, gat, half, width, at, order, gat_order):
        self.me, self.sems, self.terms, self.acc, self.inbox, self.inbox_core, self.gat = me, sems, terms, acc, inbox, inbox_core, gat
        self.width, self.order, self.gat_order = width, order, gat_order
        self.cols = pl.ds(at, width)
        self.mine = pl.ds(pl.multiple_of(me.c * half + at, 128), width)
        self.his = pl.ds(pl.multiple_of((1 - me.c) * half + at, 128), width)
        self.sent = []
        y = me.y
        a, b = y + 1 - 2 * (y % 2), 3 - y
        self.y, self.a, self.b, self.ab = y, a, b, 3 - a
        self.live = None
        self.off, self.span, self.inbox_at = 0, 256, 0
        self.steps = 1 + len(order) + len(gat_order) + 1

    def _go(self, link, pairs):
        made = [self.sems.copy(self.me, link, s, d) for s, d in pairs]
        for m in made:
            m.start()
        self.sent += made
        self.wait_for = made

    def start(self, step):
        me = self.me
        if step == 0:
            self._go("core", [(self.terms.at[:, self.his], self.inbox_core.at[:, self.cols])])
            return
        if step <= len(self.order):
            link = self.order[step - 1]
            bit = me.bit(link)
            if link[0] == "y":
                y, a, b, ab = self.y, self.a, self.b, self.ab
                if self.live is None:
                    keep, send = ([y, b], [a, ab]) if link[1] == "A" else ([y, a], [b, ab])
                else:
                    keep, send = [y], [a if link[1] == "A" else b]
                self.live = keep
                keep_off = send_off = self.off
            else:
                self.span //= 2
                live = [0, 1, 2, 3] if self.live is None else self.live
                keep = send = live
                keep_off = self.off + bit * self.span
                send_off = self.off + (1 - bit) * self.span
                self.off = keep_off
            pairs, self.adds = [], []
            for k, s in zip(keep, send, strict=True):
                box = pl.ds(self.inbox_at, self.span)
                pairs.append((self.acc.at[rows(s, send_off, self.span), self.cols], self.inbox.at[box, self.cols]))
                self.adds.append((k * 256 + keep_off, self.inbox_at, self.span))
                self.inbox_at += self.span
            self._go(link, pairs)
            return
        j = step - 1 - len(self.order)
        if j < len(self.gat_order):
            here = self.gat.at[pl.ds(pl.multiple_of(self.off, 16), self.span), self.mine]
            self._go(self.gat_order[j], [(here, here)])
            return
        here = self.gat.at[:, self.mine]
        self._go("core", [(here, here)])

    def finish(self, step):
        for m in self.wait_for:
            m.wait_recv()
        if step == 0:
            @pl.loop(0, 1024 // 64)
            def _(i):
                r = pl.ds(pl.multiple_of(i * 64, 64), 64)
                self.acc[r, self.cols] = self.terms[r, self.mine] + self.inbox_core[r, self.cols]
        elif step <= len(self.order):
            for at, box, count in self.adds:
                chunk = min(count, 64)

                @pl.loop(0, count // chunk)
                def _(i):
                    r = pl.ds(pl.multiple_of(at + i * chunk, 16), chunk)
                    q = pl.ds(pl.multiple_of(box + i * chunk, 16), chunk)
                    self.acc[r, self.cols] = self.acc[r, self.cols] + self.inbox[q, self.cols]
            if step == len(self.order):
                self.gat[pl.ds(pl.multiple_of(self.off, 16), self.span), self.mine] = self.acc[
                    rows(self.y, self.off, self.span), self.cols]
        elif step <= len(self.order) + len(self.gat_order):
            link = self.gat_order[step - 1 - len(self.order)]
            self.off = self.off - self.me.bit(link) * self.span
            self.span *= 2

    def close(self):
        for m in self.sent:
            m.wait_send()


def rotated(i):
    return tuple(LINKS[(i + j) % 6] for j in range(6))


def reduce_parts(me, sems, terms, acc, inbox, inbox_core, gat):
    cols = terms.shape[1]
    half = cols // 2
    n, starts = (6, (0, 1, 2, 3, 4, 5)) if cols == 3072 else (4, (0, 1, 3, 4))
    width = half // n
    out = []
    for i in range(n):
        order = rotated(starts[i])
        back = tuple(l for l in reversed(order) if l[0] != "y")
        out.append(Reduce(me, sems, terms, acc, inbox, inbox_core, gat, half, width, i * width, order, back))
    return out


def gather_parts(me, sems, shard, full):
    cols = full.shape[1]
    half = cols // 2
    tiles = half // 128
    plans = []
    planes = [tuple(PLANE[(i + j) % 4] for j in range(4)) for i in range(4)]
    if tiles == 12:
        at = 0
        for i in range(4):
            plans.append((256, at, (("yA", "yB") if i % 2 else ("yB", "yA")) + planes[i]))
            at += 256
        plans.append((256, at, ("yA", "yB")))
        plans.append((256, at + 256, ("yB", "yA")))
    else:
        for i in range(4):
            plans.append((128, i * 128, (("yA", "yB") if i % 2 else ("yB", "yA")) + planes[i]))
    return [Gather(me, sems, shard, full, w, me.c * half + at, order) for w, at, order in plans]


def run_lockstep(parts):
    steps = max(p.steps for p in parts)
    for s in range(steps):
        for p in parts:
            if s < p.steps:
                p.start(s)
        for p in parts:
            if s < p.steps:
                p.finish(s)
    for p in parts:
        p.close()


def gather_kernel(s0, s1, s2, s3, f0, f1, f2, f3, send, recv, local):
    me = Place()
    own = []
    for k, (s, f) in enumerate(((s0, f0), (s1, f1), (s2, f2), (s3, f3))):
        cp = pltpu.make_async_copy(s, f.at[rows(me.y, 0, 256), :], local.at[k])
        cp.start()
        own.append(cp)
    greet(me)
    sems = Sems(send, recv)
    parts = []
    for s, f in ((s0, f0), (s1, f1), (s2, f2), (s3, f3)):
        parts += gather_parts(me, sems, s, f)
    run_lockstep(parts)
    for cp in own:
        cp.wait()


def gather_weights(*shards):
    anyspec = pl.BlockSpec(memory_space=pl.ANY)
    return pl.pallas_call(
        gather_kernel,
        out_shape=[jax.ShapeDtypeStruct((1024, s.shape[1]), s.dtype) for s in shards],
        in_specs=[anyspec] * 4,
        out_specs=[anyspec] * 4,
        scratch_shapes=[pltpu.SemaphoreType.DMA((400,)), pltpu.SemaphoreType.DMA((400,)), pltpu.SemaphoreType.DMA((4,))],
        compiler_params=pltpu.CompilerParams(collective_id=1, has_side_effects=True, vmem_limit_bytes=32 << 20),
        name="gather_weights",
    )(*shards)


def reduce_kernel(scale, n, *refs):
    terms, outs = refs[:n], refs[n:2 * n]
    acc, inbox, core, gat = (refs[2 * n + i * n:3 * n + i * n] for i in range(4))
    send, recv = refs[6 * n:]
    me = Place()
    greet(me)
    sems = Sems(send, recv)
    parts = []
    for k in range(n):
        parts += reduce_parts(me, sems, terms[k], acc[k], inbox[k], core[k], gat[k])
    run_lockstep(parts)
    for k in range(n):
        @pl.loop(0, 16)
        def _(i):
            r = pl.ds(pl.multiple_of(i * 16, 16), 16)
            outs[k][r, :] = gat[k][r, :].astype(jnp.float32) * scale


def reduce_terms(scale, cid, *terms):
    n = len(terms)
    v = pl.BlockSpec(memory_space=pltpu.VMEM)
    bf = jnp.bfloat16
    scratch = [pltpu.VMEM((1024, t.shape[1] // 2), bf) for t in terms]
    scratch += [pltpu.VMEM((1024, t.shape[1] // 2), bf) for t in terms]
    scratch += [pltpu.VMEM((1024, t.shape[1] // 2), bf) for t in terms]
    scratch += [pltpu.VMEM((256, t.shape[1]), bf) for t in terms]
    return pl.pallas_call(
        functools.partial(reduce_kernel, scale, n),
        out_shape=[jax.ShapeDtypeStruct((256, t.shape[1]), jnp.float32) for t in terms],
        in_specs=[v] * n,
        out_specs=[v] * n,
        scratch_shapes=scratch + [pltpu.SemaphoreType.DMA((500,)), pltpu.SemaphoreType.DMA((500,))],
        compiler_params=pltpu.CompilerParams(collective_id=cid, has_side_effects=True, vmem_limit_bytes=60 << 20),
        name="reduce_terms",
    )(*terms)


FAR = -1e30


def heads_apart(block):
    first = lax.broadcasted_iota(jnp.int32, block.shape, 1) < 64
    zero = jnp.zeros_like(block)
    return jnp.concatenate([jnp.where(first, block, zero), jnp.where(first, zero, block)], axis=0)


def heads_together(wide):
    count = wide.shape[1] // 2
    return jnp.concatenate([wide[:64, :count], wide[64:, count:]], axis=0).T


def nt(a, b):
    return lax.dot_general(a, b, (((1,), (1,)), ((), ())), preferred_element_type=jnp.float32)


def tn(a, b):
    return lax.dot_general(a, b, (((0,), (0,)), ((), ())), preferred_element_type=jnp.float32)


def nn(a, b):
    return jnp.dot(a, b, preferred_element_type=jnp.float32)


def window_bias(key_span, query_span, low, high):
    gap = key_span - query_span
    return jnp.where((gap >= low) & (gap <= high), 0.0, FAR).astype(jnp.float32)


def prob_of(keys, queries, bias):
    score = nt(keys, queries) + jnp.concatenate([bias, bias], axis=1)
    terms = jnp.exp(score - jnp.max(score, axis=0, keepdims=True))
    return terms * (1.0 / jnp.sum(terms, axis=0, keepdims=True))


UP_BLOCKS = ((0, 0, 256), (128, 64, 320), (256, 192, 320))
DIT_BLOCKS = ((0, 0, 384), (128, 128, 384), (256, 256, 320))


def up_forward_kernel(q, k, v, kh, vh, qs, ks, live, mix, kx, vx, bias):
    @pl.when(pl.program_id(0) == 0)
    def _():
        for i, (r0, k0, n) in enumerate(UP_BLOCKS):
            bias[i, :n] = window_bias(ks[k0:k0 + n], qs[:, r0:r0 + 128], 0, 1)
    kx[:384], kx[384:] = k[...], kh[...]
    vx[:384], vx[384:] = v[...], vh[...]
    for i, (r0, k0, n) in enumerate(UP_BLOCKS):
        queries = heads_apart(q[r0:r0 + 128] * jnp.bfloat16(0.125))
        p = prob_of(kx[k0:k0 + n], queries, bias[i, :n])
        out = tn(vx[k0:k0 + n], p.astype(jnp.bfloat16))
        mix[r0:r0 + 128] = (heads_together(out) * live[r0:r0 + 128]).astype(jnp.bfloat16)


def up_backward_kernel(q, k, v, kh, vh, dm, qs, ks, dq, dk, dv, dkh, dvh, kx, vx, bias, dkx, dvx):
    @pl.when(pl.program_id(0) == 0)
    def _():
        for i, (r0, k0, n) in enumerate(UP_BLOCKS):
            bias[i, :n] = window_bias(ks[k0:k0 + n], qs[:, r0:r0 + 128], 0, 1)
    kx[:384], kx[384:] = k[...], kh[...]
    vx[:384], vx[384:] = v[...], vh[...]
    dkx[...] = jnp.zeros_like(dkx)
    dvx[...] = jnp.zeros_like(dvx)
    for i, (r0, k0, n) in enumerate(UP_BLOCKS):
        keys, values = kx[k0:k0 + n], vx[k0:k0 + n]
        queries = heads_apart(q[r0:r0 + 128] * jnp.bfloat16(0.125))
        p = prob_of(keys, queries, bias[i, :n])
        backward_block(p, p.astype(jnp.bfloat16), keys, values, queries, heads_apart(dm[r0:r0 + 128]), r0, k0, n, dq, dkx, dvx)
    dk[...], dkh[...] = dkx[:384], dkx[384:].astype(jnp.bfloat16)
    dv[...], dvh[...] = dvx[:384], dvx[384:].astype(jnp.bfloat16)


def backward_block(p, low, keys, values, queries, dout, r0, k0, n, dq, dkx, dvx):
    dp = nt(values, dout)
    ds = (p * (dp - jnp.sum(p * dp, axis=0, keepdims=True))).astype(jnp.bfloat16)
    dvx[k0:k0 + n] += nn(low, dout)
    dkx[k0:k0 + n] += nn(ds, queries)
    dq[r0:r0 + 128] = (heads_together(tn(keys, ds)) * 0.125).astype(jnp.bfloat16)


def dit_kernel(q, k, v, kh, vh, dm, qs, ks, live, mix, dq, dk, dv, dkh, dvh, kx, vx, bias, dkx, dvx):
    @pl.when(pl.program_id(0) == 0)
    def _():
        for i, (r0, k0, n) in enumerate(DIT_BLOCKS):
            bias[i, :n] = window_bias(ks[k0:k0 + n], qs[:, r0:r0 + 128], -2, 0)
    kx[:192], kx[192:] = kh[...], k[...]
    vx[:192], vx[192:] = vh[...], v[...]
    dkx[...] = jnp.zeros_like(dkx)
    dvx[...] = jnp.zeros_like(dvx)
    for i, (r0, k0, n) in enumerate(DIT_BLOCKS):
        keys, values = kx[k0:k0 + n], vx[k0:k0 + n]
        queries = heads_apart(q[r0:r0 + 128] * jnp.bfloat16(0.125))
        p = prob_of(keys, queries, bias[i, :n])
        low = p.astype(jnp.bfloat16)
        mix[r0:r0 + 128] = (heads_together(tn(values, low)) * live[r0:r0 + 128]).astype(jnp.bfloat16)
        backward_block(p, low, keys, values, queries, heads_apart(dm[r0:r0 + 128]), r0, k0, n, dq, dkx, dvx)
    dk[...], dkh[...] = dkx[192:], dkx[:192].astype(jnp.bfloat16)
    dv[...], dvh[...] = dvx[192:], dvx[:192].astype(jnp.bfloat16)


def cols(rows_, first):
    return pl.BlockSpec((rows_, 128), lambda g: (0, first + g))


def whole(shape):
    return pl.BlockSpec(shape, lambda g: (0, 0))


def attention_call(kernel, rim, name, act, halo, dmix, qs, ks, live, with_mix, with_grad):
    bf, f32 = jnp.bfloat16, jnp.float32
    ext = 384 + rim
    ins = [act, act, act, halo, halo]
    specs = [cols(384, 0), cols(384, 8), cols(384, 16), cols(rim, 0), cols(rim, 8)]
    if with_grad:
        ins.append(dmix)
        specs.append(cols(384, 0))
    ins += [qs, ks]
    specs += [whole((1, 384)), whole((ext, 1))]
    outs, ospecs = [], []
    if with_mix:
        ins.append(live)
        specs.append(whole((384, 1)))
        outs.append(jax.ShapeDtypeStruct((384, 1024), bf))
        ospecs.append(cols(384, 0))
    scratch = [pltpu.VMEM((ext, 128), bf), pltpu.VMEM((ext, 128), bf), pltpu.VMEM((3, 384, 128), f32)]
    if with_grad:
        outs += [jax.ShapeDtypeStruct((384, 1024), bf)] + [jax.ShapeDtypeStruct((384, 1024), f32)] * 2 + [jax.ShapeDtypeStruct((rim, 1024), bf)] * 2
        ospecs += [cols(384, 0)] * 3 + [cols(rim, 0)] * 2
        scratch += [pltpu.VMEM((ext, 128), f32), pltpu.VMEM((ext, 128), f32)]
    return pl.pallas_call(
        kernel, grid=(8,), in_specs=specs, out_specs=ospecs, out_shape=outs, scratch_shapes=scratch,
        cost_estimate=pl.CostEstimate(flops=8 << 30, bytes_accessed=10 << 20, transcendentals=0),
        compiler_params=pltpu.CompilerParams(vmem_limit_bytes=40 << 20), name=name,
    )(*ins)


EPS = 1e-06
DEAD = 1 << 20


def normalize_rows(xfull):
    inverse = lax.rsqrt(jnp.mean(xfull * xfull, axis=-1, keepdims=True) + EPS)
    return (xfull * inverse, inverse)


def norm_backward(xfull, inverse, d_normed):
    row_inner = jnp.mean(d_normed * xfull, axis=-1, keepdims=True)
    return inverse * d_normed - xfull * (inverse * inverse * inverse) * row_inner


def shift(block, distance):
    n = lax.axis_size("seq")
    return lax.ppermute(block, "seq", [(i - distance, i) for i in range(n) if 0 <= i - distance < n])


def term(left, right):
    return lax.dot_general(left, right, (((0,), (0,)), ((), ())), preferred_element_type=jnp.float32).astype(jnp.bfloat16)


def local(frames, valid_length, span_frames, w1_shard, p1_shard, w2_shard, p2_shard, cotangent):
    bf, f32 = jnp.bfloat16, jnp.float32
    x0, cot = frames[0], cotangent[0]
    length, span = valid_length[0], span_frames[0]
    first = lax.axis_index("seq") * 384
    here = first + jnp.arange(384, dtype=jnp.int32)
    query_span = (here // span)[None, :]
    live = (here < length).astype(f32)[:, None]

    def key_span(positions):
        alive = (positions >= 0) & (positions < length)
        return jnp.where(alive, positions // span, DEAD)[:, None]

    ahead_span = key_span(first + jnp.arange(512, dtype=jnp.int32))
    behind_span = key_span(first - 192 + jnp.arange(576, dtype=jnp.int32))

    w1, p1, w2, p2 = gather_weights(w1_shard, p1_shard, w2_shard, p2_shard)

    x0f = x0.astype(f32)
    n0f, inv0 = normalize_rows(x0f)
    n0 = n0f.astype(bf)
    act1 = nn(n0, w1).astype(bf)
    halo1 = shift(act1[:128, 1024:], -1)
    (mix1,) = attention_call(up_forward_kernel, 128, "up_forward", act1, halo1, None, query_span, ahead_span, live, True, False)
    hidden = (x0f + nn(mix1, p1)).astype(bf)
    hf = hidden.astype(f32)
    n1f, inv1 = normalize_rows(hf)
    n1 = n1f.astype(bf)
    act2 = nn(n1, w2).astype(bf)
    halo2 = shift(act2[192:, 1024:], 1)
    dmix2 = (nt(cot, p2) * live).astype(bf)
    mix2, dq2, dk2, dv2, dkh2, dvh2 = attention_call(
        dit_kernel, 192, "dit", act2, halo2, dmix2, query_span, behind_span, live, True, True)
    result = (hf + nn(mix2, p2)).astype(bf)
    gp2 = term(mix2, cot)
    back2 = shift(jnp.concatenate([dkh2, dvh2], axis=1), -1).astype(f32)
    late = jnp.pad(back2, ((192, 0), (0, 0)))
    dact2 = jnp.concatenate([dq2, (dk2 + late[:, :1024]).astype(bf), (dv2 + late[:, 1024:]).astype(bf)], axis=1)
    gw2 = term(n1, dact2)
    dhidden = (cot.astype(f32) + norm_backward(hf, inv1, nt(dact2, w2))).astype(bf)
    dmix1 = (nt(dhidden, p1) * live).astype(bf)
    gp1 = term(mix1, dhidden)
    dq1, dk1, dv1, dkh1, dvh1 = attention_call(
        up_backward_kernel, 128, "up_backward", act1, halo1, dmix1, query_span, ahead_span, live, False, True)
    back1 = shift(jnp.concatenate([dkh1, dvh1], axis=1), 1).astype(f32)
    early = jnp.pad(back1, ((0, 256), (0, 0)))
    dact1 = jnp.concatenate([dq1, (dk1 + early[:, :1024]).astype(bf), (dv1 + early[:, 1024:]).astype(bf)], axis=1)
    gw1 = term(n0, dact1)
    dframes = (dhidden.astype(f32) + norm_backward(x0f, inv0, nt(dact1, w1))).astype(bf)
    scale = float(8 * 6144) ** -0.5
    tw1, tp1, tw2, tp2 = reduce_terms(scale, 2, gw1, gp1, gw2, gp2)
    return (result[None], dframes[None], tw1, tp1, tw2, tp2)


def solution(mesh):
    rows3, row, flat = P(("fsdp", "dp"), "seq", None), P("fsdp", None), P(("fsdp", "dp"))
    return jax.shard_map(
        local, mesh=mesh, in_specs=(rows3, flat, flat, row, row, row, row, rows3),
        out_specs=(rows3, rows3, row, row, row, row), check_vma=False)
```

time: 665 us -> 342 us (0.51)
  waiting for transfers between devices: 301 us -> 17.5 us
  Pallas kernels: 0 us -> 237 us
  matrix products: 251 us -> 35.9 us
  starting transfers between devices: 25.1 us -> 8.96 us
  local copies, waits for them, and re-layouts: 38.5 us -> 22.6 us
  between operations: 16.2 us -> 2.66 us
  other arithmetic: 23.1 us -> 11.5 us
    pallas_call x0 -> x5, Pallas kernels: none -> 237 us  [the longest x1 111 us: reduce_terms(): pl.pallas_call(functools.partial(reduce_kernel, scale, n), out_shape=[jax...]
    dot_general x22 -> x12, matrix products: 232 us -> 35.9 us  [the longest x4 16.8 us: term(): lax.dot_general(left, right, (((0,), (0,)), ((), ())), preferred_element_...]
    all_gather x4 -> x0, waiting for transfers between devices: 120 us -> none  [the longest x1 64.5 us: local(): lax.all_gather(upsampler_inproj, 'fsdp', axis=0, tiled=True)]
    psum x1 -> x0, waiting for transfers between devices: 105 us -> none  [local(): lax.psum(shares[0].astype(jnp.bfloat16), ('seq', 'dp')).astype(jnp.float32)]
    reduce_scatter x4 -> x0, waiting for transfers between devices: 65 us -> none  [the longest x1 65 us: local(): lax.psum_scatter(upsampler_inproj_partial.astype(jnp.bfloat16), 'fsdp', s...]
    sub x2 -> x0, matrix products: 19 us -> none  [attend_forward(): exp_terms = jnp.exp(scores - row_max)]
    unnamed x68, local copies, waits for them, and re-layouts: 3.18 us -> 20.7 us
    ppermute x8 -> x4, starting transfers between devices: 24.4 us -> 8.96 us  [shift(): lax.ppermute(block, 'seq', [(i - distance, i) for i in range(n) if 0 <= i...]
  transfers between devices with their start and end apart: 17 -> 4, of which waited for: 7 -> 3; matrix products, arithmetic and copies ran while one was open for 46% -> 6% of each run, Pallas kernels for 0% -> 0%
where the time goes in v1:
time: 342 us; the launch traced here: 336 us
  Pallas kernels  237 us (69%)
  matrix products  35.9 us (10%)
  local copies, waits for them, and re-layouts  22.6 us (7%)
  waiting for transfers between devices  17.5 us (5%)
  other arithmetic  11.5 us (3%)
  starting transfers between devices  8.96 us (3%)
    pallas_call x1, Pallas kernels, reduce_terms(): pl.pallas_call(functools.partial(reduce_kernel, scale, n), out_shape=[jax...  111 us
    pallas_call x1, Pallas kernels, gather_weights(): pl.pallas_call(gather_kernel, out_shape=[jax.ShapeDtypeStruct((1024, s.sh...  77.2 us
    pallas_call x3, Pallas kernels, attention_call(): pl.pallas_call(kernel, grid=(8,), in_specs=specs, out_specs=ospecs, out_s...  48.7 us
    unnamed x68, local copies, waits for them, and re-layouts  20.7 us
    ppermute x4, waiting for transfers between devices, shift(): lax.ppermute(block, 'seq', [(i - distance, i) for i in range(n) if 0 <= i...  17.5 us
    dot_general x4, matrix products, term(): lax.dot_general(left, right, (((0,), (0,)), ((), ())), preferred_element_...  16.8 us
    dot_general x4, matrix products, nt(): lax.dot_general(a, b, (((1,), (1,)), ((), ())), preferred_element_type=jn...  10.4 us
    ppermute x4, starting transfers between devices, shift(): lax.ppermute(block, 'seq', [(i - distance, i) for i in range(n) if 0 <= i...  8.96 us
  transfers between devices with their start and end apart: 4, of which 3 were waited for; matrix products, arithmetic and copies ran while one was open for 6% of the time, Pallas kernels for 0%

profile of v1, /device:TPU:1, one launch (start us, length us, event | category | flops | bytes accessed | tf_op | source)
XLA Modules:
  0.0 336.0 jit_solution(15640684912446443445)
XLA Ops:
  0.6 1.4 fusion.8
  2.0 1.4 copy-done
  3.4 1.4 copy-done.1
  6.9 77.2 %gather_weights.1 = (bf16[1024,3072]{1,0:T(8,128)(2,1)S(1)}, bf16[1024,1024]{1,0:T(8,128)(2,1)S(1)}, bf16[1024,3072]{1,0:T(8,128)(2,1)S(1)}, bf16[1024,1024]{1,0:T(8,128)(2,1)S(1)}) custom-call(bf16[256,3072]{1,0:T(8,128)(2,1)S(1)} %copy-done, bf16[256,1024]{1,0:T(8,128)(2,1)S(1)} %copy-done.2, bf16[256,3072]{1,0:T(8,128)(2,1)S(1)} %copy-done.1, ...), custom_call_target="tpu_custom_call" | custom-call | tf_op jit(solution)/shard_map/gather_weights/pallas_call | solution.py:278
  84.2 2.9 convolution_convert_fusion.3.q.k.v
  87.1 1.6 copy-done.7
  91.0 2.2 collective-permute-start
  94.7 2.7 fusion.36.ks
  97.4 5.8 %collective-permute-done.kh.vh = bf16[128,2048]{1,0:T(8,128)(2,1)S(1)} collective-permute-done((bf16[128,2048]{1,0:T(8,128)(2,1)}, bf16[128,2048]{1,0:T(8,128)(2,1)S(1)}, u32[]{:S(2)}, u32[]{:S(2)}) %collective-permute-start) | collective-permute-done | bytes 524320 | tf_op jit(solution)/shard_map/ppermute | solution.py:479
  103.2 9.8 %up_forward.1 = bf16[384,1024]{1,0:T(8,128)(2,1)S(1)} custom-call(bf16[384,3072]{1,0:T(8,128)(2,1)S(1)} %convolution_convert_fusion.3.q.k.v, bf16[384,3072]{1,0:T(8,128)(2,1)S(1)} %convolution_convert_fusion.3.q.k.v, bf16[384,3072]{1,0:T(8,128)(2,1)S(1)} %convolution_convert_fusion.3.q.k.v, bf16[128,2048]{1,0:T(8,128)(2,1)S(1)} %collective-permute-done.kh.vh, ...), custom_call_target="tpu_custom_call" | custom-call | flops 8589934592 | bytes 10485760 | tf_op jit(solution)/shard_map/up_forward/pallas_call | solution.py:456
  113.0 1.1 fusion
  114.2 2.9 convolution_convert_fusion.2.q.k.v
  118.1 2.5 collective-permute-start.1
  120.6 3.0 fusion.31.ks
  123.6 2.8 fusion.20.dm
  126.4 2.9 collective-permute-done.1.kh.vh
  129.2 23.7 %dit.1 = (bf16[384,1024]{1,0:T(8,128)(2,1)S(1)}, bf16[384,1024]{1,0:T(8,128)(2,1)S(1)}, f32[384,1024]{1,0:T(8,128)S(1)}, f32[384,1024]{1,0:T(8,128)S(1)}, bf16[1...) custom-call(bf16[384,3072]{1,0:T(8,128)(2,1)S(1)} %convolution_convert_fusion.2.q.k.v, ...), custom_call_target="tpu_custom_call" | custom-call | flops 8589934592 | bytes 10485760 | tf_op jit(solution)/shard_map/dit/pallas_call | solution.py:456
  153.0 2.1 collective-permute-start.2
  155.1 2.6 convolution_convert_fusion.4.refs_3_
  157.7 1.9 fusion.21
  159.6 8.9 %collective-permute-done.2 = bf16[192,2048]{1,0:T(8,128)(2,1)S(1)} collective-permute-done((bf16[192,2048]{1,0:T(8,128)(2,1)S(1)}, bf16[192,2048]{1,0:T(8,128)(2,1)S(1)}, u32[]{:S(2)}, u32[]{:S(2)}) %collective-permute-start.2) | collective-permute-done | bytes 786464 | tf_op jit(solution)/shard_map/ppermute | solution.py:479
  171.5 2.7 fusion.7
  177.4 15.2 %up_backward.1 = (bf16[384,1024]{1,0:T(8,128)(2,1)S(1)}, f32[384,1024]{1,0:T(8,128)S(1)}, f32[384,1024]{1,0:T(8,128)S(1)}, bf16[128,1024]{1,0:T(8,128)(2,1)S(1)}, bf16[128,1024]{1,0:T(8,128)(2,1)S(1)}) custom-call(bf16[384,3072]{1,0:T(8,128)(2,1)S(1)} %copy-done.5, bf16[384,3072]{1,0:T(8,128)(2,1)S(1)} %copy-done.5, bf16[384,3072]{1,0:T(8,128)(2,1)S(1)} %copy-done.5, ...), custom_call_target="tpu_custom_call" | custom-call | flops 8589934592 | bytes 10485760 | tf_op jit(solution)/shard_map/up_backward/pallas_call | solution.py:456
  192.7 2.1 collective-permute-start.3
  194.8 2.6 convolution_convert_fusion.5.refs_1_
  197.5 5.8 %convolution_convert_fusion.refs_2_ = bf16[1024,3072]{1,0:T(8,128)(2,1)} fusion(bf16[384,1024]{1,0:T(8,128)(2,1)S(1)} %get-tuple-element.47, bf16[384,1024]{1,0:T(8,128)(2,1)S(1)} %get-tuple-element.46, bf16[384,1024]{1,0:T(8,128)(2,1)S(1)} %get-tuple-element.30, bf16[384,1024]{1,0:T(8,128)(2,1)S(1)} %copy-done.25, f32[384]{0:T(512)S(1)} %get-tuple-element.51), kind=kOutput, calls=%fused_computation | convolution fusion | flops 2427322368 | bytes 9438720 | tf_op jit(solution)/shard_map/dot_general | solution.py:483
  206.3 3.8 %fusion.15 = (f32[384]{0:T(512)S(1)}, f32[384,1024]{1,0:T(8,128)}) fusion(bf16[1,384,1024]{2,1,0:T(8,128)(2,1)S(1)} %copy-done.19, bf16[1024,3072]{1,0:T(8,128)(2,1)S(1)} %bitcast.46, bf16[384,1024]{1,0:T(8,128)(2,1)S(1)} %get-tuple-element.45, bf16[384,1024]{1,0:T(8,128)(2,1)S(1)} %get-tuple-element.44, bf16[384,1024]{1,0:T(8,128)(2,1)S(1)} %get-tuple-element.35), kind=kOutput, calls=%fused_computation.33 | convolution fusion | flops 2424176128 | bytes 11011584 | tf_op jit(solution)/shard_map/dot_general | solution.py:341
  210.2 5.8 %convolution_convert_fusion.1.refs_0_ = bf16[1024,3072]{1,0:T(8,128)(2,1)} fusion(bf16[384,1024]{1,0:T(8,128)(2,1)S(1)} %get-tuple-element.45, bf16[384,1024]{1,0:T(8,128)(2,1)S(1)} %get-tuple-element.44, bf16[384,1024]{1,0:T(8,128)(2,1)S(1)} %get-tuple-element.35, bf16[1,384,1024]{2,1,0:T(8,128)(2,1)S(1)} %copy-done.19, f32[384]{0:T(512)S(1)} %get-tuple-element.49), kind=kOutput, calls=%fused_computation.1 | convolution fusion | flops 2427322368 | bytes 9438720 | tf_op jit(solution)/shard_map/dot_general | solution.py:483
  216.0 111.0 %reduce_terms.1 = (f32[256,3072]{1,0:T(8,128)}, f32[256,1024]{1,0:T(8,128)}, f32[256,3072]{1,0:T(8,128)}, f32[256,1024]{1,0:T(8,128)}) custom-call(bf16[1024,3072]{1,0:T(8,128)(2,1)} %convolution_convert_fusion.1.refs_0_, bf16[1024,1024]{1,0:T(8,128)(2,1)} %convolution_convert_fusion.5.refs_1_, bf16[1024,3072]{1,0:T(8,128)(2,1)} %convolution_convert_fusion.refs_2_, ...), custom_call_target="tpu_custom_call" | custom-call | tf_op jit(solution)/shard_map/reduce_terms/pallas_call | solution.py:315
  326.9 1.4 fusion.24
  329.1 1.7 copy.22
  332.8 1.7 copy.24
  (84 shorter events, 19.0 us)
Async XLA Ops:
  2.0 1.4 copy-start
  6.9 77.3 %copy-start.17 = (bf16[1,384,1024]{2,1,0:T(8,128)(2,1)S(1)}, bf16[1,384,1024]{2,1,0:T(8,128)(2,1)}, u32[]{:S(2)}) copy-start(bf16[1,384,1024]{2,1,0:T(8,128)(2,1)} %param.8) | copy-start | bytes 2359300
  84.2 3.0 copy-start.6
  84.2 4.5 %copy-start.7 = (bf16[1024,3072]{1,0:T(8,128)(2,1)}, bf16[1024,3072]{1,0:T(8,128)(2,1)S(1)}, u32[]{:S(2)}) copy-start(bf16[1024,3072]{1,0:T(8,128)(2,1)S(1)} %get-tuple-element.27) | copy-start | bytes 18874372
  84.2 5.3 %copy-start.8 = (bf16[1024,1024]{1,0:T(8,128)(2,1)}, bf16[1024,1024]{1,0:T(8,128)(2,1)S(1)}, u32[]{:S(2)}) copy-start(bf16[1024,1024]{1,0:T(8,128)(2,1)S(1)} %get-tuple-element.26) | copy-start | bytes 6291460
  84.2 5.9 %copy-start.11 = (bf16[1024,1024]{1,0:T(8,128)(2,1)}, bf16[1024,1024]{1,0:T(8,128)(2,1)S(1)}, u32[]{:S(2)}) copy-start(bf16[1024,1024]{1,0:T(8,128)(2,1)S(1)} %get-tuple-element.28) | copy-start | bytes 6291460
  90.1 22.9 %copy-start.4 = (bf16[384,3072]{1,0:T(8,128)(2,1)}, bf16[384,3072]{1,0:T(8,128)(2,1)S(1)}, u32[]{:S(2)}) copy-start(bf16[384,3072]{1,0:T(8,128)(2,1)S(1)} %convolution_convert_fusion.3.q.k.v) | copy-start | bytes 7077892
  91.0 12.2 %collective-permute-start = (bf16[128,2048]{1,0:T(8,128)(2,1)}, bf16[128,2048]{1,0:T(8,128)(2,1)S(1)}, u32[]{:S(2)}, u32[]{:S(2)}) collective-permute-start(bf16[128,2048]{1,0:T(8,128)(2,1)} %slice.24), channel_id=1, source_target_pairs={{8,0},{16,8},{24,16},{32,24},{40,32},{48,40},{56,48},{64,56},{72,6... | collective-permute-start | bytes 1572872 | tf_op jit(solution)/shard_map/ppermute | solution.py:479
  94.7 19.5 %slice-start.2 = ((s8[6291456]{0:T(1024)(128)(4,1)}), s8[4194304]{0:T(1024)(128)(4,1)S(1)}, s32[]{:S(2)}) async-start(s8[6291456]{0:T(1024)(128)(4,1)} %bitcast.47), calls=%async_computation.2 | async-start | bytes 8388608
  97.4 15.7 %copy-start.9 = (bf16[1024,1024]{1,0:T(8,128)(2,1)S(1)}, bf16[1024,1024]{1,0:T(8,128)(2,1)}, u32[]{:S(2)}) copy-start(bf16[1024,1024]{1,0:T(8,128)(2,1)} %copy-done.8) | copy-start | bytes 6291460
  97.4 15.6 %copy-start.18 = (bf16[1,384,1024]{2,1,0:T(8,128)(2,1)S(1)}, bf16[1,384,1024]{2,1,0:T(8,128)(2,1)}, u32[]{:S(2)}) copy-start(bf16[1,384,1024]{2,1,0:T(8,128)(2,1)} %param.8) | copy-start | bytes 2359300
  97.4 16.8 %slice-start.3 = ((s8[6291456]{0:T(1024)(128)(4,1)}), s8[2097152]{0:T(1024)(128)(4,1)S(1)}, s32[]{:S(2)}) async-start(s8[6291456]{0:T(1024)(128)(4,1)} %bitcast.47), calls=%async_computation.3 | async-start | bytes 4194304
  114.2 3.0 copy-start.24
  118.1 11.1 %collective-permute-start.1 = (bf16[192,2048]{1,0:T(8,128)(2,1)}, bf16[192,2048]{1,0:T(8,128)(2,1)}, u32[]{:S(2)}, u32[]{:S(2)}) collective-permute-start(bf16[192,2048]{1,0:T(8,128)(2,1)} %slice.25), channel_id=1, source_target_pairs={{0,8},{8,16},{16,24},{24,32},{32,40},{40,48},{48,56},{56,64},{64,7... | collective-permute-start | bytes 2359304 | tf_op jit(solution)/shard_map/ppermute | solution.py:479
  126.3 28.7 %copy-start.23 = (bf16[1,384,1024]{2,1,0:T(8,128)(2,1)S(1)}, bf16[1,384,1024]{2,1,0:T(8,128)(2,1)}, u32[]{:S(2)}) copy-start(bf16[1,384,1024]{2,1,0:T(8,128)(2,1)} %param.15) | copy-start | bytes 2359300
  153.0 15.5 %collective-permute-start.2 = (bf16[192,2048]{1,0:T(8,128)(2,1)S(1)}, bf16[192,2048]{1,0:T(8,128)(2,1)S(1)}, u32[]{:S(2)}, u32[]{:S(2)}) collective-permute-start(bf16[192,2048]{1,0:T(8,128)(2,1)S(1)} %pad_maximum_fusion.6), channel_id=1, source_target_pairs={{8,0},{16,8},{24,16},{32,24},{40,32},{48,40},{56,48},{64,56},{72,6... | collective-permute-start | bytes 2359304 | tf_op jit(solution)/shard_map/ppermute | solution.py:479
  155.1 2.7 copy-start.12
  155.1 2.6 copy-start.25
  168.5 2.2 slice-start.4
  168.9 2.6 slice-start.5
  174.2 1.6 copy-start.10
  175.8 1.7 copy-start.5
  177.4 17.4 %copy-start.14 = (bf16[384,1024]{1,0:T(8,128)(2,1)S(1)}, bf16[384,1024]{1,0:T(8,128)(2,1)}, u32[]{:S(2)}) copy-start(bf16[384,1024]{1,0:T(8,128)(2,1)} %copy-done.13) | copy-start | bytes 2359300
  192.7 10.6 %collective-permute-start.3 = (bf16[128,2048]{1,0:T(8,128)(2,1)S(1)}, bf16[128,2048]{1,0:T(8,128)(2,1)S(1)}, u32[]{:S(2)}, u32[]{:S(2)}) collective-permute-start(bf16[128,2048]{1,0:T(8,128)(2,1)S(1)} %pad_maximum_fusion.7), channel_id=1, source_target_pairs={{0,8},{8,16},{16,24},{24,32},{32,40},{40,48},{48,56},{56,64},{64,7... | collective-permute-start | bytes 1572872 | tf_op jit(solution)/shard_map/ppermute | solution.py:479
  203.3 2.2 slice-start
  203.6 2.6 slice-start.1
  203.6 2.7 copy-start.19
  216.0 111.0 %copy-start.20 = (f32[384,1024]{1,0:T(8,128)S(1)}, f32[384,1024]{1,0:T(8,128)}, u32[]{:S(2)}) copy-start(f32[384,1024]{1,0:T(8,128)} %get-tuple-element.57) | copy-start | bytes 4718596
  326.9 2.2 copy-start.16
  329.1 2.0 copy-start.22
  329.1 3.7 %copy-start.15 = (f32[256,3072]{1,0:T(8,128)S(1)}, f32[256,3072]{1,0:T(8,128)}, u32[]{:S(2)}) copy-start(f32[256,3072]{1,0:T(8,128)} %get-tuple-element.68) | copy-start | bytes 9437188
  332.8 2.0 copy-start.21
  (4 other events, 4.6 us)

commit v2 on v1

--- a/solution.py
+++ b/solution.py
@@ -1,4 +1,5 @@
 import functools
+import heapq
 import jax
 import jax.numpy as jnp
 from jax import lax
@@ -13,6 +14,7 @@
 class Place:
     def __init__(self):
         seq = lax.axis_index("seq")
+        self.seq = seq
         self.y = lax.axis_index("fsdp")
         self.zl = lax.axis_index("dp")
         self.x = seq // 4
@@ -28,20 +30,26 @@
         x, y, z, c = self.x, self.y, self.z, self.c
         if link == "core":
             c = 1 - c
+        elif link in ("next", "previous"):
+            pass
         elif link[0] == "x":
             x = 3 - x if link[1] == "B" else x + 1 - 2 * (x % 2)
         elif link[0] == "y":
             y = 3 - y if link[1] == "B" else y + 1 - 2 * (y % 2)
         else:
             z = 3 - z if link[1] == "B" else z + 1 - 2 * (z % 2)
+        if link == "next":
+            return {"seq": (self.seq + 1) % 16, "fsdp": y, "dp": self.zl}
+        if link == "previous":
+            return {"seq": (self.seq + 15) % 16, "fsdp": y, "dp": self.zl}
         return {"seq": x * 4 + (z // 2) * 2 + c, "fsdp": y, "dp": z % 2}
 
 
-def greet(me):
+def greet(me, *more):
     barrier = pltpu.get_barrier_semaphore()
-    for link in LINKS + ("core",):
+    for link in LINKS + ("core",) + more:
         pl.semaphore_signal(barrier, inc=1, device_id=me.peer(link), device_id_type=pl.DeviceIdType.MESH)
-    pl.semaphore_wait(barrier, 7)
+    pl.semaphore_wait(barrier, 7 + len(more))
 
 
 class Sems:
@@ -64,6 +72,7 @@
     def __init__(self, me, sems, shard, full, width, at, order):
         self.me, self.sems, self.shard, self.full, self.order = me, sems, shard, full, order
         self.cols = pl.ds(pl.multiple_of(at, 128), width)
+        self.width = width
         self.sent = []
         y = me.y
         self.a, self.b = y + 1 - 2 * (y % 2), 3 - y
@@ -103,6 +112,10 @@
         else:
             self._go("core", [(self.blk(k), self.blk(k)) for k in (self.a, self.b, self.ab)])
 
+    def load(self, step):
+        blocks = 1 if step == 0 else 2 if step == 1 else 3
+        return (self.order + ("core",))[step], blocks * self.span * self.width * 2, 0.0
+
     def finish(self, step):
         for m in self.wait_for:
             m.wait_recv()
@@ -117,19 +130,20 @@
 
 
 class Reduce:
-    def __init__(self, me, sems, terms, acc, inbox, inbox_core, gat, half, width, at, order, gat_order):
-        self.me, self.sems, self.terms, self.acc, self.inbox, self.inbox_core, self.gat = me, sems, terms, acc, inbox, inbox_core, gat
-        self.width, self.order, self.gat_order = width, order, gat_order
+    def __init__(self, me, sems, source, acc, inbox, inbox_core, gat, width, at, gat_at, order, ready=None):
+        self.me, self.sems, self.source, self.acc, self.inbox, self.inbox_core, self.gat = me, sems, source, acc, inbox, inbox_core, gat
+        self.width, self.order, self.ready = width, order, ready
+        self.back = tuple(l for l in reversed(order) if l[0] != "y")
         self.cols = pl.ds(at, width)
-        self.mine = pl.ds(pl.multiple_of(me.c * half + at, 128), width)
-        self.his = pl.ds(pl.multiple_of((1 - me.c) * half + at, 128), width)
+        self.mine = pl.ds(pl.multiple_of(gat_at, 128), width)
         self.sent = []
         y = me.y
         a, b = y + 1 - 2 * (y % 2), 3 - y
         self.y, self.a, self.b, self.ab = y, a, b, 3 - a
         self.live = None
         self.off, self.span, self.inbox_at = 0, 256, 0
-        self.steps = 1 + len(order) + len(gat_order) + 1
+        self.steps = 12
+        self.left = 1024
 
     def _go(self, link, pairs):
         made = [self.sems.copy(self.me, link, s, d) for s, d in pairs]
@@ -138,12 +152,21 @@
         self.sent += made
         self.wait_for = made
 
+    def load(self, step):
+        line = 2 * self.width
+        if step == 0:
+            return "core", 1024 * line, 1024 * line / 1.5e6
+        if step <= 6:
+            return self.order[step - 1], (512 >> (step - 1)) * line, (512 >> (step - 1)) * line / 1.5e6 + 0.1
+        if step <= 10:
+            return self.back[step - 7], (16 << (step - 7)) * line, 0.0
+        return "core", 256 * line, 0.0
+
     def start(self, step):
         me = self.me
         if step == 0:
-            self._go("core", [(self.terms.at[:, self.his], self.inbox_core.at[:, self.cols])])
-            return
-        if step <= len(self.order):
+            self._go("core", [(self.source, self.inbox_core.at[:, self.cols])])
+        elif step <= 6:
             link = self.order[step - 1]
             bit = me.bit(link)
             if link[0] == "y":
@@ -156,8 +179,7 @@
                 keep_off = send_off = self.off
             else:
                 self.span //= 2
-                live = [0, 1, 2, 3] if self.live is None else self.live
-                keep = send = live
+                keep = send = [0, 1, 2, 3] if self.live is None else self.live
                 keep_off = self.off + bit * self.span
                 send_off = self.off + (1 - bit) * self.span
                 self.off = keep_off
@@ -168,24 +190,25 @@
                 self.adds.append((k * 256 + keep_off, self.inbox_at, self.span))
                 self.inbox_at += self.span
             self._go(link, pairs)
-            return
-        j = step - 1 - len(self.order)
-        if j < len(self.gat_order):
+        elif step <= 10:
             here = self.gat.at[pl.ds(pl.multiple_of(self.off, 16), self.span), self.mine]
-            self._go(self.gat_order[j], [(here, here)])
-            return
-        here = self.gat.at[:, self.mine]
-        self._go("core", [(here, here)])
+            self._go(self.back[step - 7], [(here, here)])
+        else:
+            here = self.gat.at[:, self.mine]
+            self._go("core", [(here, here)])
 
     def finish(self, step):
         for m in self.wait_for:
             m.wait_recv()
         if step == 0:
+            if self.ready is not None:
+                self.ready()
+
             @pl.loop(0, 1024 // 64)
             def _(i):
                 r = pl.ds(pl.multiple_of(i * 64, 64), 64)
-                self.acc[r, self.cols] = self.terms[r, self.mine] + self.inbox_core[r, self.cols]
-        elif step <= len(self.order):
+                self.acc[r, self.cols] = self.acc[r, self.cols] + self.inbox_core[r, self.cols]
+        elif step <= 6:
             for at, box, count in self.adds:
                 chunk = min(count, 64)
 
@@ -194,12 +217,11 @@
                     r = pl.ds(pl.multiple_of(at + i * chunk, 16), chunk)
                     q = pl.ds(pl.multiple_of(box + i * chunk, 16), chunk)
                     self.acc[r, self.cols] = self.acc[r, self.cols] + self.inbox[q, self.cols]
-            if step == len(self.order):
+            if step == 6:
                 self.gat[pl.ds(pl.multiple_of(self.off, 16), self.span), self.mine] = self.acc[
                     rows(self.y, self.off, self.span), self.cols]
-        elif step <= len(self.order) + len(self.gat_order):
-            link = self.gat_order[step - 1 - len(self.order)]
-            self.off = self.off - self.me.bit(link) * self.span
+        elif step <= 10:
+            self.off = self.off - self.me.bit(self.back[step - 7]) * self.span
             self.span *= 2
 
     def close(self):
@@ -207,20 +229,59 @@
             m.wait_send()
 
 
+class Timeline:
+    def __init__(self):
+        self.now, self.free, self.queue, self.count, self.parts = 0.0, {}, [], 0, []
+
+    def launch(self, part, step=0):
+        if step == 0:
+            self.parts.append(part)
+        link, size, cost = part.load(step)
+        part.start(step)
+        begin = max(self.now, self.free.get(link, 0.0))
+        end = begin + size / (0.55e6 if link == "core" else 0.046e6)
+        self.free[link] = end
+        heapq.heappush(self.queue, (end + (1.0 if link == "core" else 2.0), self.count, part, step, cost))
+        self.count += 1
+
+    def _one(self):
+        end, _, part, step, cost = heapq.heappop(self.queue)
+        self.now = max(self.now, end)
+        part.finish(step)
+        self.now += cost
+        if step + 1 < part.steps:
+            self.launch(part, step + 1)
+
+    def poll(self):
+        while self.queue and self.queue[0][0] <= self.now:
+            self._one()
+
+    def work(self, what, time):
+        what()
+        self.now += time
+        self.poll()
+
+    def drain(self):
+        while self.queue:
+            self._one()
+        for part in self.parts:
+            part.close()
+
+
 def rotated(i):
     return tuple(LINKS[(i + j) % 6] for j in range(6))
 
 
-def reduce_parts(me, sems, terms, acc, inbox, inbox_core, gat):
-    cols = terms.shape[1]
-    half = cols // 2
-    n, starts = (6, (0, 1, 2, 3, 4, 5)) if cols == 3072 else (4, (0, 1, 3, 4))
+def reduce_parts(me, sems, terms, acc, inbox, inbox_core, gat, ready):
+    columns = terms.shape[1]
+    half = columns // 2
+    n, starts = (6, (0, 1, 2, 3, 4, 5)) if columns == 3072 else (4, (0, 1, 3, 4))
     width = half // n
     out = []
     for i in range(n):
-        order = rotated(starts[i])
-        back = tuple(l for l in reversed(order) if l[0] != "y")
-        out.append(Reduce(me, sems, terms, acc, inbox, inbox_core, gat, half, width, i * width, order, back))
+        source = terms.at[:, pl.ds(pl.multiple_of((1 - me.c) * half + i * width, 128), width)]
+        out.append(Reduce(me, sems, source, acc, inbox, inbox_core, gat, width, i * width, me.c * half + i * width,
+                          rotated(starts[i]), ready if i == 0 else None))
     return out
 
 
@@ -243,19 +304,6 @@
     return [Gather(me, sems, shard, full, w, me.c * half + at, order) for w, at, order in plans]
 
 
-def run_lockstep(parts):
-    steps = max(p.steps for p in parts)
-    for s in range(steps):
-        for p in parts:
-            if s < p.steps:
-                p.start(s)
-        for p in parts:
-            if s < p.steps:
-                p.finish(s)
-    for p in parts:
-        p.close()
-
-
 def gather_kernel(s0, s1, s2, s3, f0, f1, f2, f3, send, recv, local):
     me = Place()
     own = []
@@ -265,10 +313,11 @@
         own.append(cp)
     greet(me)
     sems = Sems(send, recv)
-    parts = []
+    line = Timeline()
     for s, f in ((s0, f0), (s1, f1), (s2, f2), (s3, f3)):
-        parts += gather_parts(me, sems, s, f)
-    run_lockstep(parts)
+        for part in gather_parts(me, sems, s, f):
+            line.launch(part)
+    line.drain()
     for cp in own:
         cp.wait()
 
@@ -284,43 +333,6 @@
         compiler_params=pltpu.CompilerParams(collective_id=1, has_side_effects=True, vmem_limit_bytes=32 << 20),
         name="gather_weights",
     )(*shards)
-
-
-def reduce_kernel(scale, n, *refs):
-    terms, outs = refs[:n], refs[n:2 * n]
-    acc, inbox, core, gat = (refs[2 * n + i * n:3 * n + i * n] for i in range(4))
-    send, recv = refs[6 * n:]
-    me = Place()
-    greet(me)
-    sems = Sems(send, recv)
-    parts = []
-    for k in range(n):
-        parts += reduce_parts(me, sems, terms[k], acc[k], inbox[k], core[k], gat[k])
-    run_lockstep(parts)
-    for k in range(n):
-        @pl.loop(0, 16)
-        def _(i):
-            r = pl.ds(pl.multiple_of(i * 16, 16), 16)
-            outs[k][r, :] = gat[k][r, :].astype(jnp.float32) * scale
-
-
-def reduce_terms(scale, cid, *terms):
-    n = len(terms)
-    v = pl.BlockSpec(memory_space=pltpu.VMEM)
-    bf = jnp.bfloat16
-    scratch = [pltpu.VMEM((1024, t.shape[1] // 2), bf) for t in terms]
-    scratch += [pltpu.VMEM((1024, t.shape[1] // 2), bf) for t in terms]
-    scratch += [pltpu.VMEM((1024, t.shape[1] // 2), bf) for t in terms]
-    scratch += [pltpu.VMEM((256, t.shape[1]), bf) for t in terms]
-    return pl.pallas_call(
-        functools.partial(reduce_kernel, scale, n),
-        out_shape=[jax.ShapeDtypeStruct((256, t.shape[1]), jnp.float32) for t in terms],
-        in_specs=[v] * n,
-        out_specs=[v] * n,
-        scratch_shapes=scratch + [pltpu.SemaphoreType.DMA((500,)), pltpu.SemaphoreType.DMA((500,))],
-        compiler_params=pltpu.CompilerParams(collective_id=cid, has_side_effects=True, vmem_limit_bytes=60 << 20),
-        name="reduce_terms",
-    )(*terms)
 
 
 FAR = -1e30
@@ -376,24 +388,6 @@
         p = prob_of(kx[k0:k0 + n], queries, bias[i, :n])
         out = tn(vx[k0:k0 + n], p.astype(jnp.bfloat16))
         mix[r0:r0 + 128] = (heads_together(out) * live[r0:r0 + 128]).astype(jnp.bfloat16)
-
-
-def up_backward_kernel(q, k, v, kh, vh, dm, qs, ks, dq, dk, dv, dkh, dvh, kx, vx, bias, dkx, dvx):
-    @pl.when(pl.program_id(0) == 0)
-    def _():
-        for i, (r0, k0, n) in enumerate(UP_BLOCKS):
-            bias[i, :n] = window_bias(ks[k0:k0 + n], qs[:, r0:r0 + 128], 0, 1)
-    kx[:384], kx[384:] = k[...], kh[...]
-    vx[:384], vx[384:] = v[...], vh[...]
-    dkx[...] = jnp.zeros_like(dkx)
-    dvx[...] = jnp.zeros_like(dvx)
-    for i, (r0, k0, n) in enumerate(UP_BLOCKS):
-        keys, values = kx[k0:k0 + n], vx[k0:k0 + n]
-        queries = heads_apart(q[r0:r0 + 128] * jnp.bfloat16(0.125))
-        p = prob_of(keys, queries, bias[i, :n])
-        backward_block(p, p.astype(jnp.bfloat16), keys, values, queries, heads_apart(dm[r0:r0 + 128]), r0, k0, n, dq, dkx, dvx)
-    dk[...], dkh[...] = dkx[:384], dkx[384:].astype(jnp.bfloat16)
-    dv[...], dvh[...] = dvx[:384], dvx[384:].astype(jnp.bfloat16)
 
 
 def backward_block(p, low, keys, values, queries, dout, r0, k0, n, dq, dkx, dvx):
@@ -459,6 +453,132 @@
         compiler_params=pltpu.CompilerParams(vmem_limit_bytes=40 << 20), name=name,
     )(*ins)
 
+def last_kernel(gp2, gw2, gp1, act, halo, dm, dh, x0, inv, n0t, w1, qs, ks,
+                dframes, t1, tp1, t2, tp2,
+                acc1, accp1, acc2, accp2, in1, inp1, in2, inp2, co1, cop1, co2, cop2,
+                outbox, kx, vx, bias, dkx, dvx, edge, hout, hin, dact, dcat, dn, send, recv, local):
+    me = Place()
+    bf = jnp.bfloat16
+    sems = Sems(send, recv)
+    loads = []
+    for i, (t, acc) in enumerate(((gp2, accp2), (gw2, acc2), (gp1, accp1))):
+        half = t.shape[1] // 2
+        cp = pltpu.make_async_copy(t.at[:, pl.ds(pl.multiple_of(me.c * half, 128), half)], acc, local.at[i])
+        cp.start()
+        loads.append(cp)
+    for i, (r0, k0, n) in enumerate(UP_BLOCKS):
+        bias[i, :n] = window_bias(ks[k0:k0 + n], qs[:, r0:r0 + 128], 0, 1)
+    greet(me, "next", "previous")
+    line = Timeline()
+    for i, (t, acc, box, core, gat) in enumerate(((gp2, accp2, inp2, cop2, tp2), (gw2, acc2, in2, co2, t2), (gp1, accp1, inp1, cop1, tp1))):
+        for part in reduce_parts(me, sems, t, acc, box, core, gat, loads[i].wait):
+            line.launch(part)
+
+    flights = {}
+
+    def attend(k):
+        @pl.loop(2 * k, 2 * k + 2)
+        def _(g):
+            at = pl.multiple_of(g * 128, 128)
+            q_at, k_at, v_at = pl.ds(at, 128), pl.ds(at + 1024, 128), pl.ds(at + 2048, 128)
+            kx[:384], kx[384:] = act[:, k_at], halo[:, q_at]
+            vx[:384], vx[384:] = act[:, v_at], halo[:, k_at]
+            dkx[...] = jnp.zeros_like(dkx)
+            dvx[...] = jnp.zeros_like(dvx)
+            for i, (r0, k0, n) in enumerate(UP_BLOCKS):
+                keys, values = kx[k0:k0 + n], vx[k0:k0 + n]
+                queries = heads_apart(act[r0:r0 + 128, q_at] * jnp.bfloat16(0.125))
+                p = prob_of(keys, queries, bias[i, :n])
+                dout = heads_apart(dm[r0:r0 + 128, q_at])
+                dp = nt(values, dout)
+                ds = (p * (dp - jnp.sum(p * dp, axis=0, keepdims=True))).astype(bf)
+                dvx[k0:k0 + n] += nn(p.astype(bf), dout)
+                dkx[k0:k0 + n] += nn(ds, queries)
+                dact[r0:r0 + 128, q_at] = (heads_together(tn(keys, ds)) * 0.125).astype(bf)
+            for full, c_at, e_at in ((dkx, k_at, q_at), (dvx, v_at, k_at)):
+                edge[:, e_at] = full[:128]
+                dact[128:, c_at] = full[128:384].astype(bf)
+                hout[:, e_at] = full[384:].astype(bf)
+
+        made = []
+        for first in (0, 1024):
+            c = pl.ds(first + 256 * k, 256)
+            made.append(sems.copy(me, "next", hout.at[:, c], hin.at[:, c]))
+        for m in made:
+            m.start()
+        flights[k] = made
+
+    def settle(k):
+        for m in flights[k]:
+            m.wait_recv()
+        for first in (0, 1024):
+            c = pl.ds(first + 256 * k, 256)
+            dact[:128, pl.ds(1024 + first + 256 * k, 256)] = (edge[:, c] + hin[:, c].astype(jnp.float32)).astype(bf)
+        for which in range(3):
+            mine = pl.ds(pl.multiple_of(which * 1024 + (2 * k + me.c) * 128, 128), 128)
+            his = pl.ds(pl.multiple_of(which * 1024 + (2 * k + 1 - me.c) * 128, 128), 128)
+            dcat[:, which * 128:which * 128 + 128] = dact[:, mine]
+            dcat[:, 384 + which * 128:512 + which * 128] = dact[:, his]
+
+        @pl.loop(0, 4)
+        def _(i):
+            r = pl.ds(pl.multiple_of(i * 256, 256), 256)
+            t = nn(n0t[r, :], dcat[...]).astype(bf)
+            acc1[r, k * 384:k * 384 + 384] = t[:, :384]
+            outbox[r, k * 384:k * 384 + 384] = t[:, 384:]
+
+    def send_terms(k):
+        for which in range(3):
+            at = k * 384 + which * 128
+            line.launch(Reduce(me, sems, outbox.at[:, pl.ds(at, 128)], acc1, in1, co1, t1, 128, at,
+                               which * 1024 + (2 * k + me.c) * 128, rotated(which + 3 * (k % 2))))
+
+    def back_to_normed():
+        @pl.loop(0, 4)
+        def _(i):
+            r = pl.ds(pl.multiple_of(i * 256, 256), 256)
+            dn[:, r] = nt(dact[...], w1[r, :])
+
+    def back_to_frames():
+        @pl.loop(0, 6)
+        def _(i):
+            r = pl.ds(pl.multiple_of(i * 64, 64), 64)
+            x = x0[r, :].astype(jnp.float32)
+            inverse = inv[r, :]
+            dframes[r, :] = (dh[r, :].astype(jnp.float32) + norm_backward(x, inverse, dn[r, :])).astype(bf)
+
+    line.work(lambda: attend(0), 4.0)
+    for k in range(1, 4):
+        line.work(lambda: attend(k), 4.0)
+        line.work(lambda: settle(k - 1), 1.2)
+        send_terms(k - 1)
+    line.work(lambda: settle(3), 1.2)
+    send_terms(3)
+    line.work(back_to_normed, 3.5)
+    line.work(back_to_frames, 1.0)
+    line.drain()
+    for made in flights.values():
+        for m in made:
+            m.wait_send()
+
+
+def last_part(*args):
+    bf, f32 = jnp.bfloat16, jnp.float32
+    v, h = pl.BlockSpec(memory_space=pltpu.VMEM), pl.BlockSpec(memory_space=pl.ANY)
+    s = lambda shape, dt=bf: pltpu.VMEM(shape, dt)
+    sizes = (3072, 1024, 3072, 1024)
+    scratch = [s((1024, c // 2)) for _ in range(3) for c in sizes]
+    scratch += [s((1024, 1536)), s((512, 128)), s((512, 128)), s((3, 384, 128), f32), s((512, 128), f32), s((512, 128), f32),
+                s((128, 2048), f32), s((128, 2048)), s((128, 2048)), s((384, 3072)), s((384, 768)), s((384, 1024), f32),
+                pltpu.SemaphoreType.DMA((520,)), pltpu.SemaphoreType.DMA((520,)), pltpu.SemaphoreType.DMA((3,))]
+    return pl.pallas_call(
+        last_kernel,
+        out_shape=[jax.ShapeDtypeStruct((384, 1024), bf)] + [jax.ShapeDtypeStruct((256, c), bf) for c in sizes],
+        in_specs=[h] * 3 + [v] * 10, out_specs=[v] * 5, scratch_shapes=scratch,
+        compiler_params=pltpu.CompilerParams(collective_id=2, has_side_effects=True, vmem_limit_bytes=60 << 20),
+        name="last_part",
+    )(*args)
+
 
 EPS = 1e-06
 DEAD = 1 << 20
@@ -525,16 +645,9 @@
     dhidden = (cot.astype(f32) + norm_backward(hf, inv1, nt(dact2, w2))).astype(bf)
     dmix1 = (nt(dhidden, p1) * live).astype(bf)
     gp1 = term(mix1, dhidden)
-    dq1, dk1, dv1, dkh1, dvh1 = attention_call(
-        up_backward_kernel, 128, "up_backward", act1, halo1, dmix1, query_span, ahead_span, live, False, True)
-    back1 = shift(jnp.concatenate([dkh1, dvh1], axis=1), 1).astype(f32)
-    early = jnp.pad(back1, ((0, 256), (0, 0)))
-    dact1 = jnp.concatenate([dq1, (dk1 + early[:, :1024]).astype(bf), (dv1 + early[:, 1024:]).astype(bf)], axis=1)
-    gw1 = term(n0, dact1)
-    dframes = (dhidden.astype(f32) + norm_backward(x0f, inv0, nt(dact1, w1))).astype(bf)
     scale = float(8 * 6144) ** -0.5
-    tw1, tp1, tw2, tp2 = reduce_terms(scale, 2, gw1, gp1, gw2, gp2)
-    return (result[None], dframes[None], tw1, tp1, tw2, tp2)
+    dframes, *totals = last_part(gp2, gw2, gp1, act1, halo1, dmix1, dhidden, x0, inv0, n0.T, w1, query_span, ahead_span)
+    return (result[None], dframes[None], *(t.astype(f32) * scale for t in totals))
 
 
 def solution(mesh):

time: 342 us -> 296 us (0.87)
  Pallas kernels: 237 us -> 198 us
  waiting for transfers between devices: 17.5 us -> 9.07 us
  other arithmetic: 11.5 us -> 17.5 us
  matrix products: 35.9 us -> 32.4 us
    pallas_call x3 -> x2, Pallas kernels: 48.7 us -> 33 us  [attention_call(): pl.pallas_call(kernel, grid=(8,), in_specs=specs, out_specs=ospecs, out_s...]
    pallas_call x1, Pallas kernels: 77.2 us -> 62.6 us  [gather_weights(): pl.pallas_call(gather_kernel, out_shape=[jax.ShapeDtypeStruct((1024, s.sh...]
    ppermute x4 -> x3, waiting for transfers between devices: 17.5 us -> 9.07 us  [shift(): lax.ppermute(block, 'seq', [(i - distance, i) for i in range(n) if 0 <= i...]
    pallas_call x1, Pallas kernels: 111 us -> 103 us  [last_part(): pl.pallas_call(last_kernel, out_shape=[jax.ShapeDtypeStruct((384, 1024),...]
    mul x0 -> x2, other arithmetic: none -> 6.5 us  [local(): t.astype(f32) * scale]
    dot_general x4 -> x3, matrix products: 16.8 us -> 13.4 us  [term(): lax.dot_general(left, right, (((0,), (0,)), ((), ())), preferred_element_...]
    dot_general x4 -> x3, matrix products: 10.4 us -> 7.76 us  [nt(): lax.dot_general(a, b, (((1,), (1,)), ((), ())), preferred_element_type=jn...]
    ppermute x4 -> x3, starting transfers between devices: 8.96 us -> 6.65 us  [shift(): lax.ppermute(block, 'seq', [(i - distance, i) for i in range(n) if 0 <= i...]
  transfers between devices with their start and end apart: 4 -> 3, of which waited for: 3 -> 2; matrix products, arithmetic and copies ran while one was open for 6% -> 8% of each run, Pallas kernels for 0% -> 0%
where the time goes in v2:
time: 296 us; the launch traced here: 290 us
  Pallas kernels  198 us (67%)
  matrix products  32.4 us (11%)
  local copies, waits for them, and re-layouts  23.6 us (8%)
  other arithmetic  17.5 us (6%)
  waiting for transfers between devices  9.07 us (3%)
  starting transfers between devices  6.65 us (2%)
  between operations  3 us (1%)
    pallas_call x1, Pallas kernels, last_part(): pl.pallas_call(last_kernel, out_shape=[jax.ShapeDtypeStruct((384, 1024),...  103 us
    pallas_call x1, Pallas kernels, gather_weights(): pl.pallas_call(gather_kernel, out_shape=[jax.ShapeDtypeStruct((1024, s.sh...  62.6 us
    pallas_call x2, Pallas kernels, attention_call(): pl.pallas_call(kernel, grid=(8,), in_specs=specs, out_specs=ospecs, out_s...  33 us
    unnamed x92, local copies, waits for them, and re-layouts  20.6 us
    dot_general x3, matrix products, term(): lax.dot_general(left, right, (((0,), (0,)), ((), ())), preferred_element_...  13.4 us
    dot_general x4, matrix products, nn(): return jnp.dot(a, b, preferred_element_type=jnp.float32)  11.3 us
    ppermute x3, waiting for transfers between devices, shift(): lax.ppermute(block, 'seq', [(i - distance, i) for i in range(n) if 0 <= i...  9.07 us
    dot_general x3, matrix products, nt(): lax.dot_general(a, b, (((1,), (1,)), ((), ())), preferred_element_type=jn...  7.76 us
  transfers between devices with their start and end apart: 3, of which 2 were waited for; matrix products, arithmetic and copies ran while one was open for 8% of the time, Pallas kernels for 0%

profile of v2, /device:TPU:1, one launch (start us, length us, event | category | flops | bytes accessed | tf_op | source)
XLA Modules:
  0.0 290.3 jit_solution(2627233771837667447)
XLA Ops:
  0.7 1.6 copy.24
  2.6 1.4 copy-done.3
  5.0 62.6 %gather_weights.1 = (bf16[1024,3072]{1,0:T(8,128)(2,1)S(1)}, bf16[1024,1024]{1,0:T(8,128)(2,1)S(1)}, bf16[1024,3072]{1,0:T(8,128)(2,1)S(1)}, bf16[1024,1024]{1,0:T(8,128)(2,1)S(1)}) custom-call(bf16[256,3072]{1,0:T(8,128)(2,1)S(1)} %copy-done.2, bf16[256,1024]{1,0:T(8,128)(2,1)S(1)} %copy-done.6, bf16[256,3072]{1,0:T(8,128)(2,1)S(1)} %copy-done.3, ...), custom_call_target="tpu_custom_call" | custom-call | tf_op jit(solution)/shard_map/gather_weights/pallas_call | solution.py:327
  67.6 1.4 copy-done.14
  69.0 1.4 copy-done.17
  70.4 2.9 convolution_convert_fusion.2.q.k.v.act
  73.3 1.6 copy-done.13
  74.9 2.4 collective-permute-start
  78.9 2.7 fusion.27.ks
  81.6 5.3 %collective-permute-done.kh.vh.halo = bf16[128,2048]{1,0:T(8,128)(2,1)S(1)} collective-permute-done((bf16[128,2048]{1,0:T(8,128)(2,1)S(1)}, bf16[128,2048]{1,0:T(8,128)(2,1)S(1)}, u32[]{:S(2)}, u32[]{:S(2)}) %collective-permute-start) | collective-permute-done | bytes 524320 | tf_op jit(solution)/shard_map/ppermute | solution.py:599
  86.9 9.8 %up_forward.1 = bf16[384,1024]{1,0:T(8,128)(2,1)S(1)} custom-call(bf16[384,3072]{1,0:T(8,128)(2,1)S(1)} %convolution_convert_fusion.2.q.k.v.act, bf16[384,3072]{1,0:T(8,128)(2,1)S(1)} %convolution_convert_fusion.2.q.k.v.act, bf16[384,3072]{1,0:T(8,128)(2,1)S(1)} %convolution_convert_fusion.2.q.k.v.act, ...), custom_call_target="tpu_custom_call" | custom-call | flops 8589934592 | bytes 10485760 | tf_op jit(solution)/shard_map/up_forward/pallas_call | solution.py:450
  96.8 1.3 fusion.3
  98.3 2.9 convolution_convert_fusion.1.q.k.v
  102.1 1.4 copy-done.8
  103.5 2.1 collective-permute-start.1
  105.6 3.0 %fusion.22.ks = s32[576,1]{1,0:T(8,128)S(1)} fusion(s32[]{:T(128)} %bitcast.45, s32[]{:T(128)S(6)} %sign.42, s32[]{:T(128)} %bitcast.41, s32[]{:T(128)S(6)} %sub.26), kind=kLoop, calls=%fused_computation.45 | loop fusion | flops 7488 | bytes 2320 | tf_op jit(solution)/shard_map/jit(_where)/select_n | solution.py:617
  108.6 2.3 fusion.13.dm
  110.9 3.7 %collective-permute-done.1.kh.vh = bf16[192,2048]{1,0:T(8,128)(2,1)S(1)} collective-permute-done((bf16[192,2048]{1,0:T(8,128)(2,1)}, bf16[192,2048]{1,0:T(8,128)(2,1)S(1)}, u32[]{:S(2)}, u32[]{:S(2)}) %collective-permute-start.1) | collective-permute-done | bytes 786464 | tf_op jit(solution)/shard_map/ppermute | solution.py:599
  116.7 23.2 %dit.1 = (bf16[384,1024]{1,0:T(8,128)(2,1)S(1)}, bf16[384,1024]{1,0:T(8,128)(2,1)S(1)}, f32[384,1024]{1,0:T(8,128)S(1)}, f32[384,1024]{1,0:T(8,128)S(1)}, bf16[1...) custom-call(bf16[384,3072]{1,0:T(8,128)(2,1)S(1)} %copy-done.9, bf16[384,3072]{1,0:T(8,128)(2,1)S(1)} %copy-done.9, ...), custom_call_target="tpu_custom_call" | custom-call | flops 8589934592 | bytes 10485760 | tf_op jit(solution)/shard_map/dit/pallas_call | solution.py:450
  141.0 2.1 collective-permute-start.2
  144.3 2.3 copy.26
  147.4 4.2 %fusion.14 = bf16[1,384,1024]{1,2,0:T(8,128)(2,1)} fusion(bf16[384,1024]{1,0:T(8,128)(2,1)} %copy-done.23, bf16[1024,1024]{1,0:T(8,128)(2,1)} %copy-done.17, bf16[384,1024]{0,1:T(8,128)(2,1)} %copy-done.34), kind=kOutput, calls=%fused_computation.35 | convolution fusion | flops 806486016 | bytes 4456448 | tf_op jit(solution)/shard_map/dot_general | solution.py:361
  151.6 2.3 copy.34
  153.8 4.0 %convolution_convert_fusion.4.gp2 = bf16[1024,1024]{1,0:T(8,128)(2,1)} fusion(bf16[384,1024]{1,0:T(8,128)(2,1)} %copy-done.23, bf16[1,384,1024]{2,1,0:T(8,128)(2,1)} %param.15), kind=kOutput, calls=%fused_computation.15 | convolution fusion | flops 806354944 | bytes 3670016 | tf_op jit(solution)/shard_map/dot_general | solution.py:603
  157.8 1.6 pad_convert_fusion
  162.1 3.4 %fusion.10 = (f32[384]{0:T(512)S(1)}, f32[384,1024]{0,1:T(8,128)S(1)}) fusion(bf16[384,1024]{0,1:T(8,128)(2,1)S(1)} %copy-done.35, bf16[1024,3072]{1,0:T(8,128)(2,1)S(1)} %bitcast.49, bf16[384,1024]{1,0:T(8,128)(2,1)S(1)} %get-tuple-element.49, bf16[384,1024]{1,0:T(8,128)(2,1)S(1)} %get-tuple-element.48, bf16[384,1024]{1,0:T(8,128)(2,1)S(1)} %copy-done.25), kind=kOutput, calls=%fused_computation.26 | convolution fusion | flops 2424176128 | bytes 11011584 | tf_op jit(solution)/shard_map/dot_general | solution.py:353
  167.2 2.0 multiply_convert_fusion.dm
  169.2 2.7 convolution_convert_fusion.3.gp1
  173.1 6.7 %convolution_convert_fusion.gw2 = bf16[1024,3072]{1,0:T(8,128)(2,1)} fusion(bf16[384,1024]{1,0:T(8,128)(2,1)} %copy-done.39, bf16[384,1024]{1,0:T(8,128)(2,1)S(1)} %copy-done.38, bf16[384,1024]{1,0:T(8,128)(2,1)S(1)} %copy-done.26, bf16[384,1024]{0,1:T(8,128)(2,1)S(1)} %copy-done.36, f32[384]{0:T(512)S(1)} %get-tuple-element.51), kind=kOutput, calls=%fused_computation | convolution fusion | flops 2427322368 | bytes 9438720 | tf_op jit(solution)/shard_map/dot_general | solution.py:603
  179.8 102.6 %last_part.1 = (bf16[384,1024]{1,0:T(8,128)(2,1)}, bf16[256,3072]{1,0:T(8,128)(2,1)}, bf16[256,1024]{1,0:T(8,128)(2,1)}, bf16[256,3072]{1,0:T(8,128)(2,1)}, bf16[256,1024]{1,0:T(8,128)(2,1)}) custom-call(bf16[1024,1024]{1,0:T(8,128)(2,1)} %convolution_convert_fusion.4.gp2, bf16[1024,3072]{1,0:T(8,128)(2,1)} %convolution_convert_fusion.gw2, ...), custom_call_target="tpu_custom_call" | custom-call | tf_op jit(solution)/shard_map/last_part/pallas_call | solution.py:574
  282.4 3.0 %convert_multiply_fusion.8 = (f32[256,1024]{1,0:T(8,128)}, f32[256,1024]{1,0:T(8,128)}) fusion(bf16[256,1024]{1,0:T(8,128)(2,1)} %get-tuple-element.35, bf16[256,1024]{1,0:T(8,128)(2,1)} %get-tuple-element.33), kind=kLoop, calls=%fused_computation.36 | loop fusion | flops 1048576 | bytes 3145728 | tf_op jit(solution)/shard_map/mul | solution.py:650
  285.3 3.5 %convert_multiply_fusion = (f32[256,3072]{1,0:T(8,128)}, f32[256,3072]{1,0:T(8,128)}) fusion(bf16[256,3072]{1,0:T(8,128)(2,1)S(1)} %copy-done.32, bf16[256,3072]{1,0:T(8,128)(2,1)S(1)} %copy-done.31), kind=kLoop, calls=%fused_computation.3 | loop fusion | flops 3145728 | bytes 9437184 | tf_op jit(solution)/shard_map/mul | solution.py:650
  (102 shorter events, 13.9 us)
Async XLA Ops:
  2.3 68.1 %copy-start.27 = (bf16[1,384,1024]{1,2,0:T(8,128)(2,1)}, bf16[1,384,1024]{1,2,0:T(8,128)(2,1)S(1)}, u32[]{:S(2)}) copy-start(bf16[1,384,1024]{1,2,0:T(8,128)(2,1)S(1)} %copy.24) | copy-start | bytes 2359300
  70.4 2.9 copy-start
  70.4 4.5 %copy-start.13 = (bf16[1024,3072]{1,0:T(8,128)(2,1)}, bf16[1024,3072]{1,0:T(8,128)(2,1)S(1)}, u32[]{:S(2)}) copy-start(bf16[1024,3072]{1,0:T(8,128)(2,1)S(1)} %get-tuple-element.23) | copy-start | bytes 18874372
  74.9 21.9 %copy-start.1 = (bf16[384,3072]{1,0:T(8,128)(2,1)}, bf16[384,3072]{1,0:T(8,128)(2,1)S(1)}, u32[]{:S(2)}) copy-start(bf16[384,3072]{1,0:T(8,128)(2,1)S(1)} %convolution_convert_fusion.2.q.k.v.act) | copy-start | bytes 7077892
  74.9 12.0 %collective-permute-start = (bf16[128,2048]{1,0:T(8,128)(2,1)S(1)}, bf16[128,2048]{1,0:T(8,128)(2,1)S(1)}, u32[]{:S(2)}, u32[]{:S(2)}) collective-permute-start(bf16[128,2048]{1,0:T(8,128)(2,1)S(1)} %slice.16), channel_id=1, source_target_pairs={{8,0},{16,8},{24,16},{32,24},{40,32},{48,40},{56,48},{64,56},{72,6... | collective-permute-start | bytes 1572872 | tf_op jit(solution)/shard_map/ppermute | solution.py:599
  78.8 35.8 %copy-start.12 = (s32[1,384]{1,0:T(1,128)}, s32[1,384]{1,0:T(1,128)S(1)}, u32[]{:S(2)}) copy-start(s32[1,384]{1,0:T(1,128)S(1)} %and_select_fusion.qs) | copy-start | bytes 4612
  78.9 19.4 %slice-start = ((s8[6291456]{0:T(1024)(128)(4,1)}), s8[4194304]{0:T(1024)(128)(4,1)S(1)}, s32[]{:S(2)}) async-start(s8[6291456]{0:T(1024)(128)(4,1)} %bitcast.46), calls=%async_computation | async-start | bytes 8388608
  78.9 17.9 %copy-start.10 = (f32[384,1]{1,0:T(8,128)}, f32[384,1]{1,0:T(8,128)S(1)}, u32[]{:S(2)}) copy-start(f32[384,1]{1,0:T(8,128)S(1)} %fusion.32.live) | copy-start | bytes 4612
  81.6 15.2 %copy-start.4 = (s32[512,1]{1,0:T(8,128)}, s32[512,1]{1,0:T(8,128)S(1)}, u32[]{:S(2)}) copy-start(s32[512,1]{1,0:T(8,128)S(1)} %fusion.27.ks) | copy-start | bytes 6148
  81.6 15.2 %copy-start.15 = (bf16[1024,1024]{1,0:T(8,128)(2,1)S(1)}, bf16[1024,1024]{1,0:T(8,128)(2,1)}, u32[]{:S(2)}) copy-start(bf16[1024,1024]{1,0:T(8,128)(2,1)} %copy-done.14) | copy-start | bytes 6291460
  81.6 15.2 %copy-start.28 = (bf16[1,384,1024]{1,2,0:T(8,128)(2,1)S(1)}, bf16[1,384,1024]{1,2,0:T(8,128)(2,1)}, u32[]{:S(2)}) copy-start(bf16[1,384,1024]{1,2,0:T(8,128)(2,1)} %copy-done.27) | copy-start | bytes 2359300
  81.6 16.6 %slice-start.1 = ((s8[6291456]{0:T(1024)(128)(4,1)}), s8[2097152]{0:T(1024)(128)(4,1)S(1)}, s32[]{:S(2)}) async-start(s8[6291456]{0:T(1024)(128)(4,1)} %bitcast.46), calls=%async_computation.1 | async-start | bytes 4194304
  86.9 9.9 %copy-start.5 = (bf16[128,2048]{1,0:T(8,128)(2,1)}, bf16[128,2048]{1,0:T(8,128)(2,1)S(1)}, u32[]{:S(2)}) copy-start(bf16[128,2048]{1,0:T(8,128)(2,1)S(1)} %collective-permute-done.kh.vh.halo) | copy-start | bytes 1572868
  98.2 2.9 %copy-start.34 = (bf16[384,1024]{0,1:T(8,128)(2,1)}, bf16[384,1024]{0,1:T(8,128)(2,1)S(1)}, u32[]{:S(2)}) copy-start(bf16[384,1024]{0,1:T(8,128)(2,1)S(1)} %get-tuple-element.53) | copy-start | bytes 2359300
  98.2 10.3 %copy-start.18 = (bf16[1024,1024]{1,0:T(8,128)(2,1)S(1)}, bf16[1024,1024]{1,0:T(8,128)(2,1)}, u32[]{:S(2)}) copy-start(bf16[1024,1024]{1,0:T(8,128)(2,1)} %copy-done.17) | copy-start | bytes 6291460
  103.5 11.1 %collective-permute-start.1 = (bf16[192,2048]{1,0:T(8,128)(2,1)}, bf16[192,2048]{1,0:T(8,128)(2,1)S(1)}, u32[]{:S(2)}, u32[]{:S(2)}) collective-permute-start(bf16[192,2048]{1,0:T(8,128)(2,1)} %slice.17), channel_id=1, source_target_pairs={{0,8},{8,16},{16,24},{24,32},{32,40},{40,48},{48,56},{56,64},{64,7... | collective-permute-start | bytes 2359304 | tf_op jit(solution)/shard_map/ppermute | solution.py:599
  108.6 6.9 %copy-start.9 = (bf16[384,3072]{1,0:T(8,128)(2,1)S(1)}, bf16[384,3072]{1,0:T(8,128)(2,1)}, u32[]{:S(2)}) copy-start(bf16[384,3072]{1,0:T(8,128)(2,1)} %copy-done.8) | copy-start | bytes 7077892
  108.6 6.9 %copy-start.11 = (f32[384,1]{1,0:T(8,128)S(1)}, f32[384,1]{1,0:T(8,128)}, u32[]{:S(2)}) copy-start(f32[384,1]{1,0:T(8,128)} %copy-done.10) | copy-start | bytes 4612
  139.9 3.3 %copy-start.24 = (bf16[384,1024]{1,0:T(8,128)(2,1)}, bf16[384,1024]{1,0:T(8,128)(2,1)S(1)}, u32[]{:S(2)}) copy-start(bf16[384,1024]{1,0:T(8,128)(2,1)S(1)} %get-tuple-element.26) | copy-start | bytes 2359300
  139.9 3.3 %copy-start.29 = (bf16[1,384,1024]{1,2,0:T(8,128)(2,1)S(1)}, bf16[1,384,1024]{1,2,0:T(8,128)(2,1)}, u32[]{:S(2)}) copy-start(bf16[1,384,1024]{1,2,0:T(8,128)(2,1)} %copy-done.27) | copy-start | bytes 2359300
  141.0 16.8 %collective-permute-start.2 = (bf16[192,2048]{1,0:T(8,128)(2,1)}, bf16[192,2048]{1,0:T(8,128)(2,1)}, u32[]{:S(2)}, u32[]{:S(2)}) collective-permute-start(bf16[192,2048]{1,0:T(8,128)(2,1)} %pad_maximum_fusion.3), channel_id=1, source_target_pairs={{8,0},{16,8},{24,16},{32,24},{40,32},{48,40},{56,48},{64,56},{72,6... | collective-permute-start | bytes 2359304 | tf_op jit(solution)/shard_map/ppermute | solution.py:599
  157.8 2.5 slice-start.2
  159.5 2.6 copy-start.35
  160.3 5.3 %copy-start.37 = (bf16[384,1024]{1,0:T(8,128)(2,1)}, bf16[384,1024]{1,0:T(8,128)(2,1)S(1)}, u32[]{:S(2)}) copy-start(bf16[384,1024]{1,0:T(8,128)(2,1)S(1)} %get-tuple-element.48) | copy-start | bytes 2359300
  160.3 5.3 %copy-start.39 = (bf16[384,1024]{1,0:T(8,128)(2,1)}, bf16[384,1024]{1,0:T(8,128)(2,1)S(1)}, u32[]{:S(2)}) copy-start(bf16[384,1024]{1,0:T(8,128)(2,1)S(1)} %get-tuple-element.49) | copy-start | bytes 2359300
  162.1 3.5 %copy-start.30 = (bf16[1,384,1024]{1,2,0:T(8,128)(2,1)S(1)}, bf16[1,384,1024]{1,2,0:T(8,128)(2,1)}, u32[]{:S(2)}) copy-start(bf16[1,384,1024]{1,2,0:T(8,128)(2,1)} %copy.26) | copy-start | bytes 2359300
  169.2 3.9 %copy-start.26 = (bf16[384,1024]{1,0:T(8,128)(2,1)S(1)}, bf16[384,1024]{1,0:T(8,128)(2,1)}, u32[]{:S(2)}) copy-start(bf16[384,1024]{1,0:T(8,128)(2,1)} %copy-done.24) | copy-start | bytes 2359300
  169.2 3.9 %copy-start.36 = (bf16[384,1024]{0,1:T(8,128)(2,1)S(1)}, bf16[384,1024]{0,1:T(8,128)(2,1)}, u32[]{:S(2)}) copy-start(bf16[384,1024]{0,1:T(8,128)(2,1)} %copy-done.34) | copy-start | bytes 2359300
  169.2 3.9 %copy-start.38 = (bf16[384,1024]{1,0:T(8,128)(2,1)S(1)}, bf16[384,1024]{1,0:T(8,128)(2,1)}, u32[]{:S(2)}) copy-start(bf16[384,1024]{1,0:T(8,128)(2,1)} %copy-done.37) | copy-start | bytes 2359300
  282.3 3.0 %copy-start.31 = (bf16[256,3072]{1,0:T(8,128)(2,1)S(1)}, bf16[256,3072]{1,0:T(8,128)(2,1)}, u32[]{:S(2)}) copy-start(bf16[256,3072]{1,0:T(8,128)(2,1)} %get-tuple-element.32) | copy-start | bytes 4718596
  282.4 3.0 %copy-start.32 = (bf16[256,3072]{1,0:T(8,128)(2,1)S(1)}, bf16[256,3072]{1,0:T(8,128)(2,1)}, u32[]{:S(2)}) copy-start(bf16[256,3072]{1,0:T(8,128)(2,1)} %get-tuple-element.34) | copy-start | bytes 4718596
  285.3 3.6 %copy-start.33 = (bf16[384,1024]{1,0:T(8,128)(2,1)S(1)}, bf16[384,1024]{1,0:T(8,128)(2,1)}, u32[]{:S(2)}) copy-start(bf16[384,1024]{1,0:T(8,128)(2,1)} %get-tuple-element.31) | copy-start | bytes 2359300
  (15 other events, 22.3 us)

commit v3 on v2

--- a/solution.py
+++ b/solution.py
@@ -236,6 +236,7 @@
     def launch(self, part, step=0):
         if step == 0:
             self.parts.append(part)
+            part.over = False
         link, size, cost = part.load(step)
         part.start(step)
         begin = max(self.now, self.free.get(link, 0.0))
@@ -248,6 +249,7 @@
         end, _, part, step, cost = heapq.heappop(self.queue)
         self.now = max(self.now, end)
         part.finish(step)
+        part.over = step + 1 == part.steps
         self.now += cost
         if step + 1 < part.steps:
             self.launch(part, step + 1)
@@ -260,6 +262,10 @@
         what()
         self.now += time
         self.poll()
+
+    def until(self, parts):
+        while any(not p.over for p in parts):
+            self._one()
 
     def drain(self):
         while self.queue:
@@ -304,37 +310,6 @@
     return [Gather(me, sems, shard, full, w, me.c * half + at, order) for w, at, order in plans]
 
 
-def gather_kernel(s0, s1, s2, s3, f0, f1, f2, f3, send, recv, local):
-    me = Place()
-    own = []
-    for k, (s, f) in enumerate(((s0, f0), (s1, f1), (s2, f2), (s3, f3))):
-        cp = pltpu.make_async_copy(s, f.at[rows(me.y, 0, 256), :], local.at[k])
-        cp.start()
-        own.append(cp)
-    greet(me)
-    sems = Sems(send, recv)
-    line = Timeline()
-    for s, f in ((s0, f0), (s1, f1), (s2, f2), (s3, f3)):
-        for part in gather_parts(me, sems, s, f):
-            line.launch(part)
-    line.drain()
-    for cp in own:
-        cp.wait()
-
-
-def gather_weights(*shards):
-    anyspec = pl.BlockSpec(memory_space=pl.ANY)
-    return pl.pallas_call(
-        gather_kernel,
-        out_shape=[jax.ShapeDtypeStruct((1024, s.shape[1]), s.dtype) for s in shards],
-        in_specs=[anyspec] * 4,
-        out_specs=[anyspec] * 4,
-        scratch_shapes=[pltpu.SemaphoreType.DMA((400,)), pltpu.SemaphoreType.DMA((400,)), pltpu.SemaphoreType.DMA((4,))],
-        compiler_params=pltpu.CompilerParams(collective_id=1, has_side_effects=True, vmem_limit_bytes=32 << 20),
-        name="gather_weights",
-    )(*shards)
-
-
 FAR = -1e30
 
 
@@ -376,82 +351,217 @@
 DIT_BLOCKS = ((0, 0, 384), (128, 128, 384), (256, 256, 320))
 
 
-def up_forward_kernel(q, k, v, kh, vh, qs, ks, live, mix, kx, vx, bias):
-    @pl.when(pl.program_id(0) == 0)
-    def _():
+def first_kernel(x0, cot, s0, s1, s2, s3, qs, ahead, behind, live,
+                 act1, halo1, n0t, inv0, n1t, dact, mix1, mix2, result, dh, dmix1, w1_out,
+                 w1, p1, w2, p2, n0, n1, inv1, hidden, act2, halo2, dmix2, dn, sums, hout, hin, bias1, bias2, send, recv, local):
+    me = Place()
+    bf, f32 = jnp.bfloat16, jnp.float32
+    sems = Sems(send, recv)
+    shards, fulls = (s0, s1, s2, s3), (w1, p1, w2, p2)
+    own = [pltpu.make_async_copy(s, f.at[rows(me.y, 0, 256), :], local.at[i]) for i, (s, f) in enumerate(zip(shards, fulls, strict=True))]
+    for cp in own:
+        cp.start()
+    greet(me, "next", "previous")
+    line = Timeline()
+    parts = [gather_parts(me, sems, s, f) for s, f in zip(shards, fulls, strict=True)]
+
+    def fetch(i):
+        for part in parts[i]:
+            line.launch(part)
+
+    def have(i):
+        line.until(parts[i])
+        own[i].wait()
+
+    def chunks(count, width):
+        def run(body):
+            @pl.loop(0, count)
+            def _(i):
+                body(pl.ds(pl.multiple_of(i * width, width), width))
+        return run
+
+    def normalize(source, normed, inverse):
+        @chunks(6, 64)
+        def _(r):
+            value, inv = normalize_rows(source[r, :].astype(f32))
+            normed[r, :] = value.astype(bf)
+            inverse[r, :] = inv
+
+    def turn(normed, turned):
+        @chunks(4, 256)
+        def _(c):
+            turned[c, :] = normed[:, c].T
+
+    def project(normed, weight, act, low, high):
+        @pl.loop(low, high)
+        def _(i):
+            c = pl.ds(pl.multiple_of(i * 512, 512), 512)
+            act[:, c] = nn(normed[...], weight[:, c]).astype(bf)
+
+    def heads(k, body):
+        @pl.loop(2 * k, 2 * k + 2)
+        def _(g):
+            at = pl.multiple_of(g * 128, 128)
+            body(pl.ds(at, 128), pl.ds(at + 1024, 128), pl.ds(at + 2048, 128))
+
+    def up_block(i, q_at, k_at, v_at):
+        r0, k0, n = UP_BLOCKS[i]
+        keys, values = act1[k0:min(k0 + n, 384), k_at], act1[k0:min(k0 + n, 384), v_at]
+        if i == 2:
+            keys = jnp.concatenate([keys, halo1[:, q_at]], axis=0)
+            values = jnp.concatenate([values, halo1[:, k_at]], axis=0)
+        queries = heads_apart(act1[r0:r0 + 128, q_at] * jnp.bfloat16(0.125))
+        p = prob_of(keys, queries, bias1[i, :n])
+        mix1[r0:r0 + 128, q_at] = (heads_together(tn(values, p.astype(bf))) * live[r0:r0 + 128]).astype(bf)
+
+    def up_early(k):
+        def body(*at):
+            up_block(0, *at)
+            up_block(1, *at)
+        heads(k, body)
+
+    def up_late(k):
+        heads(k, lambda *at: up_block(2, *at))
+
+    def dit_block(i, q_at, k_at, v_at):
+        r0, k0, n = DIT_BLOCKS[i]
+        keys, values = act2[max(k0 - 192, 0):k0 - 192 + n, k_at], act2[max(k0 - 192, 0):k0 - 192 + n, v_at]
+        if k0 < 192:
+            keys = jnp.concatenate([halo2[k0:, q_at], keys], axis=0)
+            values = jnp.concatenate([halo2[k0:, k_at], values], axis=0)
+        queries = heads_apart(act2[r0:r0 + 128, q_at] * jnp.bfloat16(0.125))
+        p = prob_of(keys, queries, bias2[i, :n])
+        low = p.astype(bf)
+        mix2[r0:r0 + 128, q_at] = (heads_together(tn(values, low)) * live[r0:r0 + 128]).astype(bf)
+        dout = heads_apart(dmix2[r0:r0 + 128, q_at])
+        dp = nt(values, dout)
+        ds = (p * (dp - jnp.sum(p * dp, axis=0, keepdims=True))).astype(bf)
+        dact[r0:r0 + 128, q_at] = (heads_together(tn(keys, ds)) * 0.125).astype(bf)
+        return nn(ds, queries), nn(low, dout)
+
+    def dit_early(k):
+        def body(q_at, k_at, v_at):
+            dk, dv = dit_block(2, q_at, k_at, v_at)
+            for at, d in ((q_at, dk), (k_at, dv)):
+                sums[:256, at] = jnp.zeros((256, 128), f32)
+                sums[256:, at] = d
+        heads(k, body)
+
+    flights = {}
+
+    def dit_late(k):
+        def body(q_at, k_at, v_at):
+            for i in (0, 1):
+                _, k0, n = DIT_BLOCKS[i]
+                dk, dv = dit_block(i, q_at, k_at, v_at)
+                sums[k0:k0 + n, q_at] += dk
+                sums[k0:k0 + n, k_at] += dv
+            for at, to in ((q_at, k_at), (k_at, v_at)):
+                hout[:, at] = sums[:192, at].astype(bf)
+                dact[:192, to] = sums[192:384, at].astype(bf)
+        heads(k, body)
+        flights[k] = [sems.copy(me, "previous", hout.at[:, c], hin.at[:, c]) for c in (pl.ds(256 * k, 256), pl.ds(1024 + 256 * k, 256))]
+        for m in flights[k]:
+            m.start()
+
+    def settle(k):
+        for m in flights[k]:
+            m.wait_recv()
+        for first in (256 * k, 1024 + 256 * k):
+            c = pl.ds(first, 256)
+            dact[192:, pl.ds(1024 + first, 256)] = (sums[384:, c] + hin[:, c].astype(f32)).astype(bf)
+
+    def mixed_back(grad, weight, out):
+        @chunks(4, 256)
+        def _(c):
+            out[:, c] = (nt(grad[...], weight[c, :]) * live[...]).astype(bf)
+
+    def add_mixed(base, mix, weight, out):
+        @chunks(4, 256)
+        def _(c):
+            out[:, c] = (base[:, c].astype(f32) + nn(mix[...], weight[:, c])).astype(bf)
+
+    def normed_back():
+        @chunks(4, 256)
+        def _(c):
+            dn[:, c] = nt(dact[...], w2[c, :])
+
+    def hidden_back():
+        @chunks(6, 64)
+        def _(r):
+            dh[r, :] = (cot[r, :].astype(f32) + norm_backward(hidden[r, :].astype(f32), inv1[r, :], dn[r, :])).astype(bf)
+
+    def biases():
         for i, (r0, k0, n) in enumerate(UP_BLOCKS):
-            bias[i, :n] = window_bias(ks[k0:k0 + n], qs[:, r0:r0 + 128], 0, 1)
-    kx[:384], kx[384:] = k[...], kh[...]
-    vx[:384], vx[384:] = v[...], vh[...]
-    for i, (r0, k0, n) in enumerate(UP_BLOCKS):
-        queries = heads_apart(q[r0:r0 + 128] * jnp.bfloat16(0.125))
-        p = prob_of(kx[k0:k0 + n], queries, bias[i, :n])
-        out = tn(vx[k0:k0 + n], p.astype(jnp.bfloat16))
-        mix[r0:r0 + 128] = (heads_together(out) * live[r0:r0 + 128]).astype(jnp.bfloat16)
-
-
-def backward_block(p, low, keys, values, queries, dout, r0, k0, n, dq, dkx, dvx):
-    dp = nt(values, dout)
-    ds = (p * (dp - jnp.sum(p * dp, axis=0, keepdims=True))).astype(jnp.bfloat16)
-    dvx[k0:k0 + n] += nn(low, dout)
-    dkx[k0:k0 + n] += nn(ds, queries)
-    dq[r0:r0 + 128] = (heads_together(tn(keys, ds)) * 0.125).astype(jnp.bfloat16)
-
-
-def dit_kernel(q, k, v, kh, vh, dm, qs, ks, live, mix, dq, dk, dv, dkh, dvh, kx, vx, bias, dkx, dvx):
-    @pl.when(pl.program_id(0) == 0)
-    def _():
+            bias1[i, :n] = window_bias(ahead[k0:k0 + n], qs[:, r0:r0 + 128], 0, 1)
         for i, (r0, k0, n) in enumerate(DIT_BLOCKS):
-            bias[i, :n] = window_bias(ks[k0:k0 + n], qs[:, r0:r0 + 128], -2, 0)
-    kx[:192], kx[192:] = kh[...], k[...]
-    vx[:192], vx[192:] = vh[...], v[...]
-    dkx[...] = jnp.zeros_like(dkx)
-    dvx[...] = jnp.zeros_like(dvx)
-    for i, (r0, k0, n) in enumerate(DIT_BLOCKS):
-        keys, values = kx[k0:k0 + n], vx[k0:k0 + n]
-        queries = heads_apart(q[r0:r0 + 128] * jnp.bfloat16(0.125))
-        p = prob_of(keys, queries, bias[i, :n])
-        low = p.astype(jnp.bfloat16)
-        mix[r0:r0 + 128] = (heads_together(tn(values, low)) * live[r0:r0 + 128]).astype(jnp.bfloat16)
-        backward_block(p, low, keys, values, queries, heads_apart(dm[r0:r0 + 128]), r0, k0, n, dq, dkx, dvx)
-    dk[...], dkh[...] = dkx[192:], dkx[:192].astype(jnp.bfloat16)
-    dv[...], dvh[...] = dvx[192:], dvx[:192].astype(jnp.bfloat16)
-
-
-def cols(rows_, first):
-    return pl.BlockSpec((rows_, 128), lambda g: (0, first + g))
-
-
-def whole(shape):
-    return pl.BlockSpec(shape, lambda g: (0, 0))
-
-
-def attention_call(kernel, rim, name, act, halo, dmix, qs, ks, live, with_mix, with_grad):
+            bias2[i, :n] = window_bias(behind[k0:k0 + n], qs[:, r0:r0 + 128], -2, 0)
+
+    fetch(0)
+    fetch(1)
+    line.work(lambda: normalize(x0, n0, inv0), 1.5)
+    line.work(biases, 0.7)
+    fetch(2)
+    line.work(lambda: turn(n0, n0t), 0.8)
+    have(0)
+    fetch(3)
+    keep = pltpu.make_async_copy(w1, w1_out, local.at[4])
+    keep.start()
+    line.work(lambda: project(n0, w1, act1, 2, 6), 2.0)
+    give1 = sems.copy(me, "previous", act1.at[pl.ds(0, 128), pl.ds(1024, 2048)], halo1)
+    give1.start()
+    line.work(lambda: project(n0, w1, act1, 0, 2), 1.0)
+    for k in range(4):
+        line.work(lambda: up_early(k), 1.5)
+    give1.wait_recv()
+    for k in range(4):
+        line.work(lambda: up_late(k), 0.9)
+    have(1)
+    line.work(lambda: add_mixed(x0, mix1, p1, hidden), 1.0)
+    line.work(lambda: normalize(hidden, n1, inv1), 1.2)
+    have(2)
+    line.work(lambda: project(n1, w2, act2, 2, 6), 2.0)
+    give2 = sems.copy(me, "next", act2.at[pl.ds(192, 192), pl.ds(1024, 2048)], halo2)
+    give2.start()
+    line.work(lambda: project(n1, w2, act2, 0, 2), 1.0)
+    have(3)
+    line.work(lambda: mixed_back(cot, p2, dmix2), 1.0)
+    line.drain()
+    for k in range(4):
+        dit_early(k)
+    turn(n1, n1t)
+    give2.wait_recv()
+    for k in range(4):
+        dit_late(k)
+        if k:
+            settle(k - 1)
+    add_mixed(hidden, mix2, p2, result)
+    settle(3)
+    normed_back()
+    hidden_back()
+    mixed_back(dh, p1, dmix1)
+    keep.wait()
+    for m in [give1, give2] + [m for made in flights.values() for m in made]:
+        m.wait_send()
+
+
+def first_part(*args):
     bf, f32 = jnp.bfloat16, jnp.float32
-    ext = 384 + rim
-    ins = [act, act, act, halo, halo]
-    specs = [cols(384, 0), cols(384, 8), cols(384, 16), cols(rim, 0), cols(rim, 8)]
-    if with_grad:
-        ins.append(dmix)
-        specs.append(cols(384, 0))
-    ins += [qs, ks]
-    specs += [whole((1, 384)), whole((ext, 1))]
-    outs, ospecs = [], []
-    if with_mix:
-        ins.append(live)
-        specs.append(whole((384, 1)))
-        outs.append(jax.ShapeDtypeStruct((384, 1024), bf))
-        ospecs.append(cols(384, 0))
-    scratch = [pltpu.VMEM((ext, 128), bf), pltpu.VMEM((ext, 128), bf), pltpu.VMEM((3, 384, 128), f32)]
-    if with_grad:
-        outs += [jax.ShapeDtypeStruct((384, 1024), bf)] + [jax.ShapeDtypeStruct((384, 1024), f32)] * 2 + [jax.ShapeDtypeStruct((rim, 1024), bf)] * 2
-        ospecs += [cols(384, 0)] * 3 + [cols(rim, 0)] * 2
-        scratch += [pltpu.VMEM((ext, 128), f32), pltpu.VMEM((ext, 128), f32)]
+    v, h = pl.BlockSpec(memory_space=pltpu.VMEM), pl.BlockSpec(memory_space=pl.ANY)
+    s = lambda shape, dt=bf: pltpu.VMEM(shape, dt)
+    o = lambda *shape, dt=bf: jax.ShapeDtypeStruct(shape, dt)
+    scratch = [s((1024, 3072)), s((1024, 1024)), s((1024, 3072)), s((1024, 1024)), s((384, 1024)), s((384, 1024)), s((384, 1), f32),
+               s((384, 1024)), s((384, 3072)), s((192, 2048)), s((384, 1024)), s((384, 1024), f32), s((576, 2048), f32),
+               s((192, 2048)), s((192, 2048)), s((3, 384, 128), f32), s((3, 384, 128), f32),
+               pltpu.SemaphoreType.DMA((400,)), pltpu.SemaphoreType.DMA((400,)), pltpu.SemaphoreType.DMA((5,))]
     return pl.pallas_call(
-        kernel, grid=(8,), in_specs=specs, out_specs=ospecs, out_shape=outs, scratch_shapes=scratch,
-        cost_estimate=pl.CostEstimate(flops=8 << 30, bytes_accessed=10 << 20, transcendentals=0),
-        compiler_params=pltpu.CompilerParams(vmem_limit_bytes=40 << 20), name=name,
-    )(*ins)
+        first_kernel,
+        out_shape=[o(384, 3072), o(128, 2048), o(1024, 384), o(384, 1, dt=f32), o(1024, 384), o(384, 3072)] + [o(384, 1024)] * 5 + [o(1024, 3072)],
+        in_specs=[v] * 2 + [h] * 4 + [v] * 4, out_specs=[v] * 11 + [h], scratch_shapes=scratch,
+        compiler_params=pltpu.CompilerParams(collective_id=1, has_side_effects=True, vmem_limit_bytes=60 << 20),
+        name="first_part",
+    )(*args)
+
 
 def last_kernel(gp2, gw2, gp1, act, halo, dm, dh, x0, inv, n0t, w1, qs, ks,
                 dframes, t1, tp1, t2, tp2,
@@ -594,11 +704,6 @@
     return inverse * d_normed - xfull * (inverse * inverse * inverse) * row_inner
 
 
-def shift(block, distance):
-    n = lax.axis_size("seq")
-    return lax.ppermute(block, "seq", [(i - distance, i) for i in range(n) if 0 <= i - distance < n])
-
-
 def term(left, right):
     return lax.dot_general(left, right, (((0,), (0,)), ((), ())), preferred_element_type=jnp.float32).astype(jnp.bfloat16)
 
@@ -619,34 +724,13 @@
     ahead_span = key_span(first + jnp.arange(512, dtype=jnp.int32))
     behind_span = key_span(first - 192 + jnp.arange(576, dtype=jnp.int32))
 
-    w1, p1, w2, p2 = gather_weights(w1_shard, p1_shard, w2_shard, p2_shard)
-
-    x0f = x0.astype(f32)
-    n0f, inv0 = normalize_rows(x0f)
-    n0 = n0f.astype(bf)
-    act1 = nn(n0, w1).astype(bf)
-    halo1 = shift(act1[:128, 1024:], -1)
-    (mix1,) = attention_call(up_forward_kernel, 128, "up_forward", act1, halo1, None, query_span, ahead_span, live, True, False)
-    hidden = (x0f + nn(mix1, p1)).astype(bf)
-    hf = hidden.astype(f32)
-    n1f, inv1 = normalize_rows(hf)
-    n1 = n1f.astype(bf)
-    act2 = nn(n1, w2).astype(bf)
-    halo2 = shift(act2[192:, 1024:], 1)
-    dmix2 = (nt(cot, p2) * live).astype(bf)
-    mix2, dq2, dk2, dv2, dkh2, dvh2 = attention_call(
-        dit_kernel, 192, "dit", act2, halo2, dmix2, query_span, behind_span, live, True, True)
-    result = (hf + nn(mix2, p2)).astype(bf)
+    act1, halo1, n0t, inv0, n1t, dact2, mix1, mix2, result, dhidden, dmix1, w1 = first_part(
+        x0, cot, w1_shard, p1_shard, w2_shard, p2_shard, query_span, ahead_span, behind_span, live)
     gp2 = term(mix2, cot)
-    back2 = shift(jnp.concatenate([dkh2, dvh2], axis=1), -1).astype(f32)
-    late = jnp.pad(back2, ((192, 0), (0, 0)))
-    dact2 = jnp.concatenate([dq2, (dk2 + late[:, :1024]).astype(bf), (dv2 + late[:, 1024:]).astype(bf)], axis=1)
-    gw2 = term(n1, dact2)
-    dhidden = (cot.astype(f32) + norm_backward(hf, inv1, nt(dact2, w2))).astype(bf)
-    dmix1 = (nt(dhidden, p1) * live).astype(bf)
+    gw2 = nn(n1t, dact2).astype(bf)
     gp1 = term(mix1, dhidden)
     scale = float(8 * 6144) ** -0.5
-    dframes, *totals = last_part(gp2, gw2, gp1, act1, halo1, dmix1, dhidden, x0, inv0, n0.T, w1, query_span, ahead_span)
+    dframes, *totals = last_part(gp2, gw2, gp1, act1, halo1, dmix1, dhidden, x0, inv0, n0t, w1, query_span, ahead_span)
     return (result[None], dframes[None], *(t.astype(f32) * scale for t in totals))
 
 

time: 296 us -> 266 us (0.90)
  Pallas kernels: 198 us -> 230 us
  local copies, waits for them, and re-layouts: 23.6 us -> 1.79 us
  matrix products: 32.4 us -> 12.2 us
  waiting for transfers between devices: 9.07 us -> 0 us
  starting transfers between devices: 6.65 us -> 0 us
    pallas_call x3 -> x1, Pallas kernels: 95.6 us -> 129 us  [first_part(): pl.pallas_call(first_kernel, out_shape=[o(384, 3072), o(128, 2048), o(102...]
    unnamed x92 -> x20, local copies, waits for them, and re-layouts: 20.6 us -> 1.79 us
    ppermute x3 -> x0, waiting for transfers between devices: 9.07 us -> none  [shift(): lax.ppermute(block, 'seq', [(i - distance, i) for i in range(n) if 0 <= i...]
    dot_general x3 -> x0, matrix products: 7.76 us -> none  [nt(): lax.dot_general(a, b, (((1,), (1,)), ((), ())), preferred_element_type=jn...]
    dot_general x3 -> x2, matrix products: 13.4 us -> 6.48 us  [term(): lax.dot_general(left, right, (((0,), (0,)), ((), ())), preferred_element_...]
    ppermute x3 -> x0, starting transfers between devices: 6.65 us -> none  [shift(): lax.ppermute(block, 'seq', [(i - distance, i) for i in range(n) if 0 <= i...]
    dot_general x4 -> x1, matrix products: 11.3 us -> 5.68 us  [nn(): return jnp.dot(a, b, preferred_element_type=jnp.float32)]
  transfers between devices with their start and end apart: 3 -> 0, of which waited for: 2 -> 0; matrix products, arithmetic and copies ran while one was open for 8% -> 0% of each run, Pallas kernels for 0% -> 0%
where the time goes in v3:
time: 266 us; the launch traced here: 261 us
  Pallas kernels  230 us (86%)
  other arithmetic  14.9 us (6%)
  matrix products  12.2 us (5%)
    pallas_call x1, Pallas kernels, first_part(): pl.pallas_call(first_kernel, out_shape=[o(384, 3072), o(128, 2048), o(102...  129 us
    pallas_call x1, Pallas kernels, last_part(): pl.pallas_call(last_kernel, out_shape=[jax.ShapeDtypeStruct((384, 1024),...  101 us
    select_n x2, other arithmetic, key_span(): return jnp.where(alive, positions // span, DEAD)[:, None]  7.03 us
    mul x2, other arithmetic, local(): t.astype(f32) * scale  6.5 us
    dot_general x2, matrix products, term(): lax.dot_general(left, right, (((0,), (0,)), ((), ())), preferred_element_...  6.48 us
    dot_general x1, matrix products, nn(): return jnp.dot(a, b, preferred_element_type=jnp.float32)  5.68 us

profile of v3, /device:TPU:1, one launch (start us, length us, event | category | flops | bytes accessed | tf_op | source)
XLA Modules:
  0.0 261.1 jit_solution(12815967460233628986)
XLA Ops:
  1.9 0.7 and_select_fusion.qs
  2.6 0.7 fusion.10.live
  3.3 3.4 %fusion.5.ahead.ks = s32[512,1]{1,0:T(8,128)} fusion(s32[]{:T(128)} %bitcast.18, s32[]{:T(128)S(6)} %sign.42, s32[]{:T(128)} %bitcast.13, s32[]{:T(128)S(6)} %mul.15), kind=kLoop, calls=%fused_computation.17 | loop fusion | flops 6656 | bytes 2064 | tf_op jit(solution)/shard_map/jit(_where)/select_n | solution.py:722
  6.7 3.7 %fusion.behind = s32[576,1]{1,0:T(8,128)} fusion(s32[]{:T(128)} %bitcast.19, s32[]{:T(128)S(6)} %sign.42, s32[]{:T(128)} %bitcast.14, s32[]{:T(128)S(6)} %sub.23), kind=kLoop, calls=%fused_computation.9 | loop fusion | flops 7488 | bytes 2320 | tf_op jit(solution)/shard_map/jit(_where)/select_n | solution.py:722
  10.4 0.0 copy-start.5
  10.4 129.5 %first_part.1 = (bf16[384,3072]{1,0:T(8,128)(2,1)}, bf16[128,2048]{1,0:T(8,128)(2,1)}, bf16[1024,384]{1,0:T(8,128)(2,1)}, f32[384,1]{1,0:T(8,128)}, bf16[1024,38...) custom-call(bf16[384,1024]{1,0:T(8,128)(2,1)} %bitcast.20, ...), custom_call_target="tpu_custom_call" | custom-call | tf_op jit(solution)/shard_map/first_part/pallas_call | solution.py:557
  139.8 0.0 copy-done.5
  139.9 0.0 copy-start.2
  139.9 0.0 copy-start.8
  139.9 3.9 %convolution_convert_fusion.2.gp2 = bf16[1024,1024]{1,0:T(8,128)(2,1)} fusion(bf16[384,1024]{1,0:T(8,128)(2,1)} %get-tuple-element.24, bf16[1,384,1024]{2,1,0:T(8,128)(2,1)S(1)} %copy-done.5), kind=kOutput, calls=%fused_computation.4 | convolution fusion | flops 806354944 | bytes 3670016 | tf_op jit(solution)/shard_map/dot_general | solution.py:708
  143.7 0.0 copy-done.2
  143.7 0.0 copy-done.8
  143.7 0.0 copy-start.6
  143.7 0.0 copy-start.7
  143.7 2.6 %convolution_convert_fusion.1.gp1 = bf16[1024,1024]{1,0:T(8,128)(2,1)} fusion(bf16[384,1024]{1,0:T(8,128)(2,1)S(1)} %copy-done.8, bf16[384,1024]{1,0:T(8,128)(2,1)S(1)} %copy-done.2), kind=kOutput, calls=%fused_computation.3 | convolution fusion | flops 806354944 | bytes 3670016 | tf_op jit(solution)/shard_map/dot_general | solution.py:708
  146.4 0.0 copy-done.6
  146.4 0.0 copy-done.7
  146.4 5.7 %convolution_convert_fusion.gw2 = bf16[1024,3072]{1,0:T(8,128)(2,1)} fusion(bf16[1024,384]{1,0:T(8,128)(2,1)S(1)} %copy-done.7, bf16[384,3072]{1,0:T(8,128)(2,1)S(1)} %copy-done.6), kind=kOutput, calls=%fused_computation | convolution fusion | flops 2419064832 | bytes 9437184 | tf_op jit(solution)/shard_map/dot_general | solution.py:336
  152.1 100.5 %last_part.1 = (bf16[384,1024]{1,0:T(8,128)(2,1)}, bf16[256,3072]{1,0:T(8,128)(2,1)}, bf16[256,1024]{1,0:T(8,128)(2,1)}, bf16[256,3072]{1,0:T(8,128)(2,1)}, bf16[256,1024]{1,0:T(8,128)(2,1)}) custom-call(bf16[1024,1024]{1,0:T(8,128)(2,1)} %convolution_convert_fusion.2.gp2, bf16[1024,3072]{1,0:T(8,128)(2,1)} %convolution_convert_fusion.gw2, ...), custom_call_target="tpu_custom_call" | custom-call | tf_op jit(solution)/shard_map/last_part/pallas_call | solution.py:684
  252.6 0.0 copy-start
  252.6 0.0 copy-start.1
  252.6 3.0 %convert_multiply_fusion.2 = (f32[256,1024]{1,0:T(8,128)}, f32[256,1024]{1,0:T(8,128)}) fusion(bf16[256,1024]{1,0:T(8,128)(2,1)} %get-tuple-element.39, bf16[256,1024]{1,0:T(8,128)(2,1)} %get-tuple-element.37), kind=kLoop, calls=%fused_computation.5 | loop fusion | flops 1048576 | bytes 3145728 | tf_op jit(solution)/shard_map/mul | solution.py:734
  255.6 0.0 copy-done
  255.6 0.0 copy-done.1
  255.6 0.0 copy-start.3
  255.6 0.0 copy-start.4
  255.6 3.6 %convert_multiply_fusion = (f32[256,3072]{1,0:T(8,128)}, f32[256,3072]{1,0:T(8,128)}) fusion(bf16[256,3072]{1,0:T(8,128)(2,1)S(1)} %copy-done.1, bf16[256,3072]{1,0:T(8,128)(2,1)S(1)} %copy-done), kind=kLoop, calls=%fused_computation.1 | loop fusion | flops 3145728 | bytes 9437184 | tf_op jit(solution)/shard_map/mul | solution.py:734
  259.1 0.0 copy-done.3
  259.1 0.9 copy.20
  260.0 0.0 copy-done.4
  260.0 0.9 copy.21
Async XLA Ops:
  10.4 129.5 %copy-start.5 = (bf16[1,384,1024]{2,1,0:T(8,128)(2,1)S(1)}, bf16[1,384,1024]{2,1,0:T(8,128)(2,1)}, u32[]{:S(2)}) copy-start(bf16[1,384,1024]{2,1,0:T(8,128)(2,1)} %param.15) | copy-start | bytes 2359300
  139.9 3.9 %copy-start.2 = (bf16[384,1024]{1,0:T(8,128)(2,1)S(1)}, bf16[384,1024]{1,0:T(8,128)(2,1)}, u32[]{:S(2)}) copy-start(bf16[384,1024]{1,0:T(8,128)(2,1)} %get-tuple-element.28.dh) | copy-start | bytes 2359300
  139.9 3.9 %copy-start.8 = (bf16[384,1024]{1,0:T(8,128)(2,1)S(1)}, bf16[384,1024]{1,0:T(8,128)(2,1)}, u32[]{:S(2)}) copy-start(bf16[384,1024]{1,0:T(8,128)(2,1)} %get-tuple-element.27) | copy-start | bytes 2359300
  143.7 2.6 %copy-start.6 = (bf16[384,3072]{1,0:T(8,128)(2,1)S(1)}, bf16[384,3072]{1,0:T(8,128)(2,1)}, u32[]{:S(2)}) copy-start(bf16[384,3072]{1,0:T(8,128)(2,1)} %get-tuple-element.26) | copy-start | bytes 7077892
  143.7 2.6 %copy-start.7 = (bf16[1024,384]{1,0:T(8,128)(2,1)S(1)}, bf16[1024,384]{1,0:T(8,128)(2,1)}, u32[]{:S(2)}) copy-start(bf16[1024,384]{1,0:T(8,128)(2,1)} %get-tuple-element.25) | copy-start | bytes 2359300
  252.6 3.0 %copy-start = (bf16[256,3072]{1,0:T(8,128)(2,1)S(1)}, bf16[256,3072]{1,0:T(8,128)(2,1)}, u32[]{:S(2)}) copy-start(bf16[256,3072]{1,0:T(8,128)(2,1)} %get-tuple-element.36) | copy-start | bytes 4718596
  252.6 3.0 %copy-start.1 = (bf16[256,3072]{1,0:T(8,128)(2,1)S(1)}, bf16[256,3072]{1,0:T(8,128)(2,1)}, u32[]{:S(2)}) copy-start(bf16[256,3072]{1,0:T(8,128)(2,1)} %get-tuple-element.38) | copy-start | bytes 4718596
  255.6 3.6 %copy-start.3 = (bf16[384,1024]{1,0:T(8,128)(2,1)S(1)}, bf16[384,1024]{1,0:T(8,128)(2,1)}, u32[]{:S(2)}) copy-start(bf16[384,1024]{1,0:T(8,128)(2,1)} %get-tuple-element.23) | copy-start | bytes 2359300
  255.6 4.4 %copy-start.4 = (bf16[384,1024]{1,0:T(8,128)(2,1)S(1)}, bf16[384,1024]{1,0:T(8,128)(2,1)}, u32[]{:S(2)}) copy-start(bf16[384,1024]{1,0:T(8,128)(2,1)} %get-tuple-element.35) | copy-start | bytes 2359300
